TPU v7x, 256 devices: a whole 4x4x8 slice. The times are simulated.
256 devices in a mesh: shard: 16 (over z_hi, x), dp: 16 (over y, z_lo, core).
Axes of the slice: x: 4, y: 4, z: 8 (z_hi: 4, z_lo: 2; z = z_hi * 2 + z_lo), core: 2. Of those that a mesh axis runs over, the one named last changes fastest.
Arguments:
- tokens: bfloat16 [4096, 2304], P('dp'), may hold values from -6 to 6
- target: bfloat16 [4096, 2304], P('dp'), may hold values from -6 to 6
- segments: int32 [4096], P('dp'), may hold values from 0 to 1023, never falling along the last dimension, each value on 1 to 8 neighbouring positions
- gate_weight: bfloat16 [2304, 18432], P('dp', 'shard'), may hold values from -0.125 to 0.125
- up_weight: bfloat16 [2304, 18432], P('dp', 'shard'), may hold values from -0.125 to 0.125
- down_weight: bfloat16 [2304, 18432], P('dp', 'shard'), may hold values from -0.046875 to 0.046875
- vector: bfloat16 [2304, 18432], P('dp', 'shard'), may hold values from -6 to 6
- gradient: bfloat16 [2304, 18432], P('dp', 'shard'), may hold values from -6 to 6
Outputs:
- new_vector: bfloat16 [2304, 18432], P('dp', 'shard')
Inputs may be any that keep to these rules, and one draw needn't show every extreme that they name: `segments`: segment numbers never fall along the whole batch; each segment holds 1 to 8 tokens and one holds exactly 8.
All inputs are finite; a program needn't handle non-finite values.
Results may differ from a plain program's by a relative error of at most 0.03.
Values may be sent and summed in bfloat16 or wider, within the bound.
A program may use at most 64 MiB of HBM per device.

v0:
```python
import jax
import jax.numpy as jnp
from jax import lax
from jax.sharding import PartitionSpec as P

coeff_k = 0.7978845608028654
coeff_c = 0.044715
damping = 0.01
step_size = 0.8


def shifted(block, axis, distance):
    devices = range(lax.axis_size(axis))
    route = [(i - distance, i) for i in devices if i - distance in devices]
    return lax.ppermute(block, axis, route)


def gelu_parts(pre_act):
    inner_arg = coeff_k * (pre_act + coeff_c * pre_act * pre_act * pre_act)
    tanh_value = jnp.tanh(inner_arg)
    slope_term = coeff_k * (1.0 + 3.0 * coeff_c * pre_act * pre_act)
    curve_term = 6.0 * coeff_k * coeff_c * pre_act
    sech_square = 1.0 - tanh_value * tanh_value
    gelu_value = 0.5 * pre_act * (1.0 + tanh_value)
    gelu_slope = 0.5 * (1.0 + tanh_value) + 0.5 * pre_act * sech_square * slope_term
    gelu_curve = sech_square * (
        slope_term + 0.5 * pre_act * (curve_term - 2.0 * tanh_value * slope_term * slope_term)
    )
    return (gelu_value, gelu_slope, gelu_curve)


def per_device(tokens, target, segments, gate_weight, up_weight, down_weight, vector, gradient):
    tok_rows = tokens.shape[0]
    full_width = tokens.shape[1]
    inv_root = float(full_width) ** (-0.5)
    pre_gate = jnp.dot(
        tokens,
        lax.all_gather(gate_weight, "dp", axis=0, tiled=True),
        preferred_element_type=jnp.float32,
    )
    up_act = jnp.dot(
        tokens,
        lax.all_gather(up_weight, "dp", axis=0, tiled=True),
        preferred_element_type=jnp.float32,
    )
    tangent_raw = jnp.dot(
        tokens, lax.all_gather(vector, "dp", axis=0, tiled=True), preferred_element_type=jnp.float32
    )
    tangent_gate = tangent_raw * inv_root
    gelu_value, gelu_slope, gelu_curve = gelu_parts(pre_gate)
    hidden = (gelu_value * up_act).astype(jnp.bfloat16)
    tangent_hidden = (gelu_slope * tangent_gate * up_act).astype(jnp.bfloat16)
    down_full = lax.all_gather(down_weight, "dp", axis=0, tiled=True)
    stacked = jnp.concatenate([hidden, tangent_hidden], axis=0)
    partial_out = lax.dot_general(
        stacked, down_full, (((1,), (1,)), ((), ())), preferred_element_type=jnp.float32
    )
    last_id = segments[-1:] + 1
    before_id = shifted(last_id, "dp", 1) - 1
    previous = jnp.concatenate([before_id, segments[:-1]])
    keep_mask = (segments == previous).astype(jnp.float32)[:, None]
    summed = lax.psum(partial_out.astype(jnp.bfloat16), "shard").astype(jnp.float32)
    grad_out = (keep_mask * (summed[:tok_rows] - target.astype(jnp.float32))).astype(jnp.bfloat16)
    tangent_grad = (keep_mask * summed[tok_rows:]).astype(jnp.bfloat16)
    returned = jnp.concatenate([grad_out, tangent_grad], axis=0)
    back_hidden = jnp.dot(returned, down_full, preferred_element_type=jnp.float32)
    grad_hidden = back_hidden[:tok_rows]
    tangent_grad_hidden = back_hidden[tok_rows:]
    tangent_grad_gate = (
        up_act * (tangent_grad_hidden * gelu_slope + grad_hidden * gelu_curve * tangent_gate)
    ).astype(jnp.bfloat16)
    curvature = lax.psum_scatter(
        (
            lax.dot_general(
                tokens,
                tangent_grad_gate,
                (((0,), (0,)), ((), ())),
                preferred_element_type=jnp.float32,
            )
            * inv_root
        ).astype(jnp.bfloat16),
        "dp",
        scatter_dimension=0,
        tiled=True,
    ).astype(jnp.float32)
    updated = (
        gradient.astype(jnp.float32)
        + (1.0 - damping) * vector.astype(jnp.float32)
        - step_size * curvature
    )
    return updated.astype(jnp.bfloat16)


def solution(mesh):
    return jax.shard_map(
        per_device,
        mesh=mesh,
        in_specs=(
            P("dp", None),
            P("dp", None),
            P("dp"),
            P("dp", "shard"),
            P("dp", "shard"),
            P("dp", "shard"),
            P("dp", "shard"),
            P("dp", "shard"),
        ),
        out_specs=P("dp", "shard"),
        check_vma=False,
    )
```

profile of v0, /device:TPU:1, one launch (start us, length us, event | category | flops | bytes accessed | tf_op | source)
XLA Modules:
  0.0 476.5 jit_solution(14775815371086228619)
XLA Ops:
  6.5 0.7 all-gather.7.cloned.1.call-update
  7.3 0.7 all-gather.9.cloned.1.call-update
  8.1 0.7 all-gather.5.cloned.1.call-update
  8.8 0.5 all-gather.11.cloned.1.call-update
  9.4 46.2 %all-gather.7.cloned.1.call-done = bf16[2304,1152]{1,0:T(8,128)(2,1)} async-done(((bf16[144,1152]{1,0:T(8,128)(2,1)}), bf16[2304,1152]{1,0:T(8,128)(2,1)}) %all-gather.7.cloned.1.call-update) | async-done | bytes 5308432 | tf_op jit(solution)/shard_map/all_gather | solution.py:38
  55.6 4.2 fusion.43
  59.8 39.6 %all-gather.9.cloned.1.call-done = bf16[2304,1152]{1,0:T(8,128)(2,1)} async-done(((bf16[144,1152]{1,0:T(8,128)(2,1)}), bf16[2304,1152]{1,0:T(8,128)(2,1)}) %all-gather.9.cloned.1.call-update) | async-done | bytes 5308432 | tf_op jit(solution)/shard_map/all_gather | solution.py:47
  99.4 4.2 convolution_multiply_fusion.1
  103.6 39.6 %all-gather.5.cloned.1.call-done = bf16[2304,1152]{1,0:T(8,128)(2,1)} async-done(((bf16[144,1152]{1,0:T(8,128)(2,1)}), bf16[2304,1152]{1,0:T(8,128)(2,1)}) %all-gather.5.cloned.1.call-update) | async-done | bytes 5308432 | tf_op jit(solution)/shard_map/all_gather | solution.py:43
  143.3 6.0 %multiply_convert_fusion.1 = (bf16[256,1152]{1,0:T(8,128)(2,1)}, bf16[256,1152]{1,0:T(8,128)(2,1)}, f32[256,1152]{1,0:T(8,128)}) fusion(f32[256,1152]{1,0:T(8,128)S(1)} %fusion.43, f32[256,1152]{1,0:T(8,128)S(1)} %convolution_multiply_fusion.1, bf16[256,2304]{1,0:T(8,128)(2,1)S(1)} %copy-done, bf16[2304,1152]{1,0:T(8,128)(2,1)} %all-gather.5.cloned.1.call-done), kind=kOutput, calls=%fused_computation.37 | convolution fusion | flops 1365737472 | bytes 11206656 | tf_op jit(solution)/shard_map/dot_general | solution.py:41
  149.3 37.7 %all-gather.11.cloned.1.call-done = bf16[2304,1152]{1,0:T(8,128)(2,1)} async-done(((bf16[144,1152]{1,0:T(8,128)(2,1)}), bf16[2304,1152]{1,0:T(8,128)(2,1)}) %all-gather.11.cloned.1.call-update) | async-done | bytes 5308432 | tf_op jit(solution)/shard_map/all_gather | solution.py:53
  187.0 7.5 %convolution_convert_fusion = bf16[512,2304]{1,0:T(8,128)(2,1)} fusion(bf16[2304,1152]{1,0:T(8,128)(2,1)} %all-gather.11.cloned.1.call-done, bf16[256,1152]{1,0:T(8,128)(2,1)} %get-tuple-element.8, bf16[256,1152]{1,0:T(8,128)(2,1)} %get-tuple-element.7), kind=kOutput, calls=%fused_computation.3 | convolution fusion | flops 2721447936 | bytes 8847360 | tf_op jit(solution)/shard_map/dot_general | solution.py:55
  194.6 0.6 copy-done.4
  195.2 0.6 slice.18
  196.4 3.7 collective-permute-start
  200.8 166.5 %all-reduce.2.cloned.1.call-done = bf16[512,2304]{1,0:T(8,128)(2,1)} async-done(((bf16[512,2304]{1,0:T(8,128)(2,1)}), bf16[512,2304]{1,0:T(8,128)(2,1)}) %all-reduce.2.cloned.1.call-update) | async-done | bytes 2359312 | tf_op jit(solution)/shard_map/psum | solution.py:62
  367.3 2.1 convert_element_type.51
  369.5 0.6 fusion.4
  370.2 0.7 slice-done.1
  370.9 3.2 fusion.5
  374.2 5.1 %fusion.1 = bf16[2304,1152]{0,1:T(8,128)(2,1)} fusion(bf16[256,2304]{1,0:T(8,128)(2,1)S(1)} %copy-done, f32[256,1152]{1,0:T(8,128)S(1)} %copy-done.7, f32[256,1152]{1,0:T(8,128)S(1)} %copy-done.6, f32[512,1152]{1,0:T(8,128)S(1)} %fusion.5, f32[256,1152]{1,0:T(8,128)S(1)} %fusion.43), kind=kOutput, calls=%fused_computation.2 | convolution fusion | flops 1373405184 | bytes 12386304 | tf_op jit(solution)/shard_map/dot_general | solution.py:74
  379.2 8.6 %copy.16 = bf16[2304,1152]{1,0:T(8,128)(2,1)} copy(bf16[2304,1152]{0,1:T(8,128)(2,1)} %fusion.1) | data formatting | bytes 10616832
  387.8 80.0 %reduce-scatter.4.cloned.1.call-done = bf16[144,1152]{1,0:T(8,128)(2,1)} async-done(((bf16[2304,1152]{1,0:T(8,128)(2,1)}), bf16[144,1152]{1,0:T(8,128)(2,1)}) %reduce-scatter.4.cloned.1.call-update) | async-done | bytes 331792 | tf_op jit(solution)/shard_map/reduce_scatter | solution.py:72
  467.8 1.9 subtract_convert_fusion
  (29 shorter events, 0.5 us)
Async XLA Ops:
  6.5 49.1 %copy-start = (bf16[256,2304]{1,0:T(8,128)(2,1)S(1)}, bf16[256,2304]{1,0:T(8,128)(2,1)}, u32[]{:S(2)}) copy-start(bf16[256,2304]{1,0:T(8,128)(2,1)} %param.8) | copy-start | bytes 3538948
  6.5 49.0 %all-gather.7.cloned.1.call-start = ((), (), s32[]{:S(2)}) async-start(), calls=%async_computation.2 | async-start | bytes 5640192 | tf_op jit(solution)/shard_map/all_gather | solution.py:38
  7.3 92.2 %all-gather.9.cloned.1.call-start = ((), (), s32[]{:S(2)}) async-start(), calls=%async_computation.3 | async-start | bytes 5640192 | tf_op jit(solution)/shard_map/all_gather | solution.py:47
  8.0 135.3 %all-gather.5.cloned.1.call-start = ((), (), s32[]{:S(2)}) async-start(), calls=%async_computation.1 | async-start | bytes 5640192 | tf_op jit(solution)/shard_map/all_gather | solution.py:43
  8.7 178.2 %all-gather.11.cloned.1.call-start = ((), (), s32[]{:S(2)}) async-start(), calls=%async_computation.4 | async-start | bytes 5640192 | tf_op jit(solution)/shard_map/all_gather | solution.py:53
  9.3 358.0 %all-reduce.2.cloned.1.call-start = ((), (), s32[]{:S(2)}) async-start(), calls=%async_computation.5 | async-start | bytes 4718592 | tf_op jit(solution)/shard_map/psum | solution.py:62
  103.6 45.6 %copy-start.5 = (f32[256,1152]{1,0:T(8,128)}, f32[256,1152]{1,0:T(8,128)S(1)}, u32[]{:S(2)}) copy-start(f32[256,1152]{1,0:T(8,128)S(1)} %convolution_multiply_fusion.1) | copy-start | bytes 3538948
  194.5 0.7 copy-start.4
  194.5 273.3 %reduce-scatter.4.cloned.1.call-start = ((), (), s32[]{:S(2)}) async-start(), calls=%async_computation.6 | async-start | bytes 5640192 | tf_op jit(solution)/shard_map/reduce_scatter | solution.py:72
  196.4 3.7 collective-permute-start
  200.8 168.7 %copy-start.2 = (bf16[256,2304]{1,0:T(8,128)(2,1)S(1)}, bf16[256,2304]{1,0:T(8,128)(2,1)}, u32[]{:S(2)}) copy-start(bf16[256,2304]{1,0:T(8,128)(2,1)} %param.9) | copy-start | bytes 3538948
  367.3 2.9 slice-start
  369.5 1.4 slice-start.1
  370.9 3.2 copy-start.6
  370.9 3.2 copy-start.7
  387.8 80.0 %copy-start.1 = (bf16[144,1152]{1,0:T(8,128)(2,1)S(1)}, bf16[144,1152]{1,0:T(8,128)(2,1)}, u32[]{:S(2)}) copy-start(bf16[144,1152]{1,0:T(8,128)(2,1)} %param.14) | copy-start | bytes 995332
  387.8 80.0 %copy-start.3 = (bf16[144,1152]{1,0:T(8,128)(2,1)S(1)}, bf16[144,1152]{1,0:T(8,128)(2,1)}, u32[]{:S(2)}) copy-start(bf16[144,1152]{1,0:T(8,128)(2,1)} %param.15) | copy-start | bytes 995332
Sparse Core Ops, SparseCore 0:
  9.2 46.3 all-gather.6
  57.4 41.9 all-gather.8
  101.3 41.9 all-gather.4
  145.0 41.9 all-gather.10
  194.6 172.6 all-reduce.1
  387.9 79.8 reduce-scatter.3
where the time goes:
time: 478 us; the launch traced here: 477 us
  waiting for transfers between devices  412 us (86%)
  matrix products  30.2 us (6%)
  between operations  14.9 us (3%)
  local copies, waits for them, and re-layouts  10.6 us (2%)
    psum x1, waiting for transfers between devices, per_device(): lax.psum(partial_out.astype(jnp.bfloat16), 'shard').astype(jnp.float32)  166 us
    reduce_scatter x1, waiting for transfers between devices, per_device(): lax.psum_scatter((lax.dot_general(tokens, tangent_grad_gate, (((0,), (0,)...  80 us
    all_gather x1, waiting for transfers between devices, per_device(): lax.all_gather(gate_weight, 'dp', axis=0, tiled=True)  46.2 us
    all_gather x1, waiting for transfers between devices, per_device(): lax.all_gather(up_weight, 'dp', axis=0, tiled=True)  39.6 us
    all_gather x1, waiting for transfers between devices, per_device(): lax.all_gather(vector, 'dp', axis=0, tiled=True)  39.6 us
    all_gather x1, waiting for transfers between devices, per_device(): down_full = lax.all_gather(down_weight, 'dp', axis=0, tiled=True)  37.7 us
    unnamed x21, local copies, waits for them, and re-layouts  10 us
  transfers between devices with their start and end apart: 7, of which 6 were waited for; matrix products, arithmetic and copies ran while one was open for 3% of the time, Pallas kernels for 0%

commit v1 on v0

v1 whole, which is shorter than its diff:
```python
import functools

import jax
import jax.numpy as jnp
from jax import lax
from jax.experimental import pallas as pl
from jax.experimental.pallas import tpu as pltpu
from jax.sharding import PartitionSpec as P

MESH = pl.DeviceIdType.MESH
coeff_k = 0.7978845608028654
coeff_c = 0.044715
damping = 0.01
step_size = 0.8


def gelu_parts(pre_act):
    inner_arg = coeff_k * (pre_act + coeff_c * pre_act * pre_act * pre_act)
    tanh_value = jnp.tanh(inner_arg)
    slope_term = coeff_k * (1.0 + 3.0 * coeff_c * pre_act * pre_act)
    curve_term = 6.0 * coeff_k * coeff_c * pre_act
    sech_square = 1.0 - tanh_value * tanh_value
    gelu_value = 0.5 * pre_act * (1.0 + tanh_value)
    gelu_slope = 0.5 * (1.0 + tanh_value) + 0.5 * pre_act * sech_square * slope_term
    gelu_curve = sech_square * (
        slope_term + 0.5 * pre_act * (curve_term - 2.0 * tanh_value * slope_term * slope_term)
    )
    return (gelu_value, gelu_slope, gelu_curve)


def remote(src, dst, send_sem, recv_sem, axis, index):
    return pltpu.make_async_remote_copy(
        src_ref=src,
        dst_ref=dst,
        send_sem=send_sem,
        recv_sem=recv_sem,
        device_id={axis: index},
        device_id_type=MESH,
    )


def greet(axis, neighbours):
    barrier = pltpu.get_barrier_semaphore()
    for neighbour in neighbours:
        pl.semaphore_signal(barrier, inc=1, device_id={axis: neighbour}, device_id_type=MESH)
    pl.semaphore_wait(barrier, len(neighbours))


def dp_place():
    me = lax.axis_index("dp")
    y, zl, core = me // 4, (me // 2) % 2, me % 2

    def at(dy, dz, dc):
        return ((y + dy) % 4) * 4 + ((zl + dz) % 2) * 2 + (core + dc) % 2

    return at


GATHER_COPIES = 17


def gather_kernel(count, depth, cut, *refs):
    ins, outs = refs[:count], refs[count : 2 * count]
    send_sem, recv_sem, own_sem = refs[2 * count :]
    at = dp_place()
    sib, up, down, zed = at(0, 0, 1), at(1, 0, 0), at(-1, 0, 0), at(0, 1, 0)
    greet("dp", (sib, up, down, zed))

    def rows(w, owner, part):
        lo, size = {"w": (0, depth), "a": (0, cut), "b": (cut, depth - cut)}[part]
        return outs[w].at[pl.ds(pl.multiple_of(owner * depth + lo, 16), size)]

    me = at(0, 0, 0)
    table = [
        (me, "w", sib, at(0, 0, 1)),
        (me, "w", up, at(-1, 0, 0)),
        (me, "w", down, at(1, 0, 0)),
        (me, "w", zed, at(0, 1, 0)),
        (at(0, 1, 0), "w", up, at(-1, 1, 0)),
        (at(0, 1, 0), "w", down, at(1, 1, 0)),
        (at(0, 1, 0), "w", sib, at(0, 1, 1)),
        (at(-1, 0, 0), "a", up, at(2, 0, 0)),
        (at(1, 0, 0), "b", down, at(2, 0, 0)),
        (at(-1, 0, 0), "w", sib, at(-1, 0, 1)),
        (at(1, 0, 0), "w", sib, at(1, 0, 1)),
        (at(-1, 1, 0), "w", sib, at(-1, 1, 1)),
        (at(1, 1, 0), "w", sib, at(1, 1, 1)),
        (at(2, 0, 0), "a", zed, at(2, 1, 0)),
        (at(2, 0, 0), "b", zed, at(2, 1, 0)),
        (at(2, 0, 0), "w", sib, at(2, 0, 1)),
        (at(2, 1, 0), "w", sib, at(2, 1, 1)),
    ]
    sent = []

    def start(w, *numbers):
        for k in numbers:
            owner, part, target, _ = table[k]
            src = ins[w] if k < 4 else rows(w, owner, part)
            copy = remote(src, rows(w, owner, part), send_sem.at[w, k], recv_sem.at[w, k], "dp", target)
            copy.start()
            sent.append(copy)

    def wait(w, *numbers):
        for k in numbers:
            _, part, target, owner = table[k]
            ref = rows(w, owner, part)
            remote(ref, ref, send_sem.at[w, k], recv_sem.at[w, k], "dp", target).wait_recv()

    own = []
    for s in range(-1, count + 3):
        if s + 1 < count:
            start(s + 1, 1, 2, 3, 0)
            copy = pltpu.make_async_copy(ins[s + 1], rows(s + 1, me, "w"), own_sem.at[s + 1])
            copy.start()
            own.append(copy)
        w = s - 0
        if 0 <= w < count:
            wait(w, 3)
            start(w, 4, 5, 6)
            wait(w, 1)
            start(w, 7, 9)
            wait(w, 2)
            start(w, 8, 10)
        w = s - 1
        if 0 <= w < count:
            wait(w, 7)
            start(w, 13)
            wait(w, 8)
            start(w, 14, 15)
            wait(w, 4)
            start(w, 11)
            wait(w, 5)
            start(w, 12)
        w = s - 2
        if 0 <= w < count:
            wait(w, 13, 14)
            start(w, 16)
    for w in range(count):
        wait(w, 0, 6, 9, 10, 11, 12, 15, 16)
    for copy in own:
        copy.wait()
    for copy in sent:
        copy.wait_send()


def gather(arrays, ident):
    count, (depth, width) = len(arrays), arrays[0].shape
    cut = (depth // 32 + 1) * 16 if depth % 32 else depth // 2
    return pl.pallas_call(
        functools.partial(gather_kernel, count, depth, cut),
        out_shape=[jax.ShapeDtypeStruct((16 * depth, width), a.dtype) for a in arrays],
        in_specs=[pl.BlockSpec(memory_space=pl.ANY)] * count,
        out_specs=[pl.BlockSpec(memory_space=pl.ANY)] * count,
        scratch_shapes=[
            pltpu.SemaphoreType.DMA((count, GATHER_COPIES)),
            pltpu.SemaphoreType.DMA((count, GATHER_COPIES)),
            pltpu.SemaphoreType.DMA((count,)),
        ],
        compiler_params=pltpu.CompilerParams(collective_id=ident, has_side_effects=True),
    )(*arrays)


def plus(a, *more):
    total = a.astype(jnp.float32)
    for b in more:
        total = total + b.astype(jnp.float32)
    return total


PIECES = 3


def sum_kernel(rows, width, p_ref, o_ref, xin, xtx, xc, zin, ztx, sx, rx, sz, rz, s4, r4):
    me = lax.axis_index("shard")
    x, zh = me % 4, me // 4
    right, left = zh * 4 + (x + 1) % 4, zh * 4 + (x + 3) % 4
    above, below = ((zh + 1) % 4) * 4 + x, ((zh + 3) % 4) * 4 + x
    greet("shard", (right, left, above, below))
    quarter, piece = rows // 4, width // PIECES
    sub = quarter // 4
    sent = []

    def go(src, dst, s, r, target):
        copy = remote(src, dst, s, r, "shard", target)
        copy.start()
        sent.append(copy)

    def got(ref, s, r):
        remote(ref, ref, s, r, "shard", right).wait_recv()

    def cols(q):
        return pl.ds(q * piece, piece)

    def ring1(q, src, size, base, k, inbox, s, r, plus1, minus1):
        half = size // 2

        def part(chunk, h):
            return src(q).at[pl.ds(pl.multiple_of(base + ((k + chunk) % 4) * size + h * half, 16), half)]

        go(part(2, 1), inbox.at[q, 0], s.at[q, 0], r.at[q, 0], plus1)
        go(part(2, 0), inbox.at[q, 1], s.at[q, 1], r.at[q, 1], minus1)
        go(part(1, 0), inbox.at[q, 2], s.at[q, 2], r.at[q, 2], plus1)
        go(part(3, 1), inbox.at[q, 5], s.at[q, 5], r.at[q, 5], minus1)

    def ring2(q, src, size, base, k, inbox, out, s, r, plus1, minus1):
        half = size // 2

        def part(chunk, h):
            return src(q)[pl.ds(pl.multiple_of(base + ((k + chunk) % 4) * size + h * half, 16), half)]

        got(inbox.at[q, 0], s.at[q, 0], r.at[q, 0])
        out[q, 0] = plus(part(1, 1), inbox[q, 0]).astype(jnp.bfloat16)
        go(out.at[q, 0], inbox.at[q, 3], s.at[q, 3], r.at[q, 3], plus1)
        got(inbox.at[q, 1], s.at[q, 1], r.at[q, 1])
        out[q, 1] = plus(part(3, 0), inbox[q, 1]).astype(jnp.bfloat16)
        go(out.at[q, 1], inbox.at[q, 4], s.at[q, 4], r.at[q, 4], minus1)

    def ring3(q, src, size, base, k, inbox, s, r):
        half = size // 2
        for i in (2, 5, 3, 4):
            got(inbox.at[q, i], s.at[q, i], r.at[q, i])
        sums = []
        for h in range(2):
            mine = src(q)[pl.ds(pl.multiple_of(base + k * size + h * half, 16), half)]
            sums.append(plus(mine, inbox[q, 2 + h], inbox[q, 4 + h]))
        return sums

    def whole(q):
        return p_ref.at[:, cols(q)]

    def mine(q):
        return xc.at[q]

    def out_rows(start, size, q):
        return o_ref.at[pl.ds(pl.multiple_of(start, 16), size), cols(q)]

    def step(i, q):
        half, shalf = quarter // 2, sub // 2
        if i == 0:
            ring1(q, whole, quarter, 0, x, xin, sx, rx, right, left)
        if i == 1:
            ring2(q, whole, quarter, 0, x, xin, xtx, sx, rx, right, left)
        if i == 2:
            sums = ring3(q, whole, quarter, 0, x, xin, sx, rx)
            for h in range(2):
                xc[q, h * half : (h + 1) * half] = sums[h].astype(jnp.bfloat16)
            ring1(q, mine, sub, 0, zh, zin, sz, rz, above, below)
        if i == 3:
            ring2(q, mine, sub, 0, zh, zin, ztx, sz, rz, above, below)
        base = x * quarter
        if i == 4:
            sums = ring3(q, mine, sub, 0, zh, zin, sz, rz)
            for h in range(2):
                out_rows(base + zh * sub + h * shalf, shalf, q)[...] = sums[h].astype(jnp.bfloat16)
            ref = out_rows(base + zh * sub, sub, q)
            go(ref, ref, s4.at[q, 0], r4.at[q, 0], above)
            go(ref, ref, s4.at[q, 1], r4.at[q, 1], below)
        if i == 5:
            lo, hi = base + ((zh + 3) % 4) * sub, base + ((zh + 1) % 4) * sub
            got(out_rows(lo, sub, q), s4.at[q, 0], r4.at[q, 0])
            ref = out_rows(lo, shalf, q)
            go(ref, ref, s4.at[q, 2], r4.at[q, 2], above)
            got(out_rows(hi, sub, q), s4.at[q, 1], r4.at[q, 1])
            ref = out_rows(hi + shalf, shalf, q)
            go(ref, ref, s4.at[q, 3], r4.at[q, 3], below)
        if i == 6:
            far = base + ((zh + 2) % 4) * sub
            got(out_rows(far, shalf, q), s4.at[q, 2], r4.at[q, 2])
            got(out_rows(far + shalf, shalf, q), s4.at[q, 3], r4.at[q, 3])
            ref = out_rows(base, quarter, q)
            go(ref, ref, s4.at[q, 4], r4.at[q, 4], right)
            go(ref, ref, s4.at[q, 5], r4.at[q, 5], left)
        if i == 7:
            lo, hi = ((x + 3) % 4) * quarter, ((x + 1) % 4) * quarter
            got(out_rows(lo, quarter, q), s4.at[q, 4], r4.at[q, 4])
            ref = out_rows(lo, half, q)
            go(ref, ref, s4.at[q, 6], r4.at[q, 6], right)
            got(out_rows(hi, quarter, q), s4.at[q, 5], r4.at[q, 5])
            ref = out_rows(hi + half, half, q)
            go(ref, ref, s4.at[q, 7], r4.at[q, 7], left)
        if i == 8:
            far = ((x + 2) % 4) * quarter
            got(out_rows(far, half, q), s4.at[q, 6], r4.at[q, 6])
            got(out_rows(far + half, half, q), s4.at[q, 7], r4.at[q, 7])

    for t in range(9 + PIECES - 1):
        for q in range(PIECES):
            if 0 <= t - q < 9:
                step(t - q, q)
    for copy in sent:
        copy.wait_send()


def sum_over_shard(partial, ident):
    rows, width = partial.shape
    piece = width // PIECES
    quarter = rows // 4
    sub = quarter // 4
    bf = jnp.bfloat16
    return pl.pallas_call(
        functools.partial(sum_kernel, rows, width),
        out_shape=jax.ShapeDtypeStruct((rows, width), bf),
        in_specs=[pl.BlockSpec(memory_space=pltpu.VMEM)],
        out_specs=pl.BlockSpec(memory_space=pltpu.VMEM),
        scratch_shapes=[
            pltpu.VMEM((PIECES, 6, quarter // 2, piece), bf),
            pltpu.VMEM((PIECES, 2, quarter // 2, piece), bf),
            pltpu.VMEM((PIECES, quarter, piece), bf),
            pltpu.VMEM((PIECES, 6, sub // 2, piece), bf),
            pltpu.VMEM((PIECES, 2, sub // 2, piece), bf),
        ]
        + [pltpu.SemaphoreType.DMA((PIECES, 6))] * 4
        + [pltpu.SemaphoreType.DMA((PIECES, 8))] * 2,
        compiler_params=pltpu.CompilerParams(
            collective_id=ident, has_side_effects=True, vmem_limit_bytes=40 * 2**20
        ),
    )(partial)


PARTS = 3


def scatter_kernel(depth, cut, width, p_ref, g_ref, v_ref, o_ref, inbox, out, ss, rs):
    at = dp_place()
    up, down, zed = at(1, 0, 0), at(-1, 0, 0), at(0, 1, 0)
    greet("dp", (up, down, zed))
    part_width = width // PARTS
    sent = []

    def chip(dy, dz):
        return at(dy, dz, 0) // 2

    def cols(q):
        return pl.ds(q * part_width, part_width)

    def block(dy, dz, q, lo=0, size=depth):
        return p_ref.at[pl.ds(pl.multiple_of(chip(dy, dz) * depth + lo, 16), size), cols(q)]

    def half(slot, lo, size, q):
        return inbox.at[slot, pl.ds(lo, size), cols(q)]

    def go(src, dst, k, q, target):
        copy = remote(src, dst, ss.at[q, k], rs.at[q, k], "dp", target)
        copy.start()
        sent.append(copy)

    def got(ref, k, q):
        remote(ref, ref, ss.at[q, k], rs.at[q, k], "dp", zed).wait_recv()

    def whole(slot, q):
        return half(slot, 0, depth, q)

    rest = depth - cut

    def step(i, q):
        if i == 0:
            go(block(2, 1, q), whole(0, q), 0, q, zed)
            go(block(1, 1, q), whole(1, q), 1, q, up)
            go(block(-1, 1, q), whole(2, q), 2, q, down)
        if i == 1:
            got(whole(0, q), 0, q)
            out[0, :, cols(q)] = plus(block(2, 0, q)[...], inbox[0, :, cols(q)]).astype(jnp.bfloat16)
            go(out.at[0, pl.ds(0, cut), cols(q)], half(3, 0, cut, q), 3, q, up)
            go(out.at[0, pl.ds(cut, rest), cols(q)], half(3, cut, rest, q), 4, q, down)
            got(whole(1, q), 1, q)
            got(whole(2, q), 2, q)
            out[1, :, cols(q)] = plus(
                block(0, 1, q)[...], inbox[1, :, cols(q)], inbox[2, :, cols(q)]
            ).astype(jnp.bfloat16)
            go(out.at[1, :, cols(q)], whole(4, q), 5, q, zed)
        if i == 2:
            got(half(3, 0, cut, q), 3, q)
            out[2, :cut, cols(q)] = plus(
                block(1, 0, q, 0, cut)[...], inbox[3, :cut, cols(q)]
            ).astype(jnp.bfloat16)
            out[2, cut:, cols(q)] = block(1, 0, q, cut, rest)[...]
            go(out.at[2, :, cols(q)], whole(5, q), 6, q, up)
            got(half(3, cut, rest, q), 4, q)
            out[3, cut:, cols(q)] = plus(
                block(-1, 0, q, cut, rest)[...], inbox[3, cut:, cols(q)]
            ).astype(jnp.bfloat16)
            out[3, :cut, cols(q)] = block(-1, 0, q, 0, cut)[...]
            go(out.at[3, :, cols(q)], whole(6, q), 7, q, down)
        if i == 3:
            got(whole(4, q), 5, q)
            got(whole(5, q), 6, q)
            got(whole(6, q), 7, q)
            total = plus(
                block(0, 0, q)[...], inbox[4, :, cols(q)], inbox[5, :, cols(q)], inbox[6, :, cols(q)]
            )
            o_ref[:, cols(q)] = (
                g_ref[:, cols(q)].astype(jnp.float32)
                + (1.0 - damping) * v_ref[:, cols(q)].astype(jnp.float32)
                - step_size * total
            ).astype(jnp.bfloat16)

    for t in range(4 + PARTS - 1):
        for q in range(PARTS):
            if 0 <= t - q < 4:
                step(t - q, q)
    for copy in sent:
        copy.wait_send()


def scatter_update(partial, gradient, vector, ident):
    depth, width = gradient.shape
    cut = (depth // 32 + 1) * 16 if depth % 32 else depth // 2
    bf = jnp.bfloat16
    vmem = pl.BlockSpec(memory_space=pltpu.VMEM)
    return pl.pallas_call(
        functools.partial(scatter_kernel, depth, cut, width),
        out_shape=jax.ShapeDtypeStruct((depth, width), bf),
        in_specs=[vmem] * 3,
        out_specs=vmem,
        scratch_shapes=[
            pltpu.VMEM((7, depth, width), bf),
            pltpu.VMEM((4, depth, width), bf),
            pltpu.SemaphoreType.DMA((PARTS, 8)),
            pltpu.SemaphoreType.DMA((PARTS, 8)),
        ],
        compiler_params=pltpu.CompilerParams(
            collective_id=ident, has_side_effects=True, vmem_limit_bytes=40 * 2**20
        ),
    )(partial, gradient, vector)


def shifted(block, axis, distance):
    devices = range(lax.axis_size(axis))
    route = [(i - distance, i) for i in devices if i - distance in devices]
    return lax.ppermute(block, axis, route)


def swapped(block):
    return lax.ppermute(block, "dp", [(i, i ^ 1) for i in range(16)])


def per_device(tokens, target, segments, gate_weight, up_weight, down_weight, vector, gradient):
    tok_rows, full_width = tokens.shape
    depth = gate_weight.shape[0]
    inv_root = float(full_width) ** (-0.5)
    core = lax.axis_index("dp") % 2
    other_tokens = swapped(tokens)
    last_id = segments[-1:] + 1
    before_id = shifted(last_id, "dp", 1) - 1
    gate_full, up_full, vector_full, down_full = gather(
        (gate_weight, up_weight, vector, down_weight), 1
    )
    pre_gate = jnp.dot(tokens, gate_full, preferred_element_type=jnp.float32)
    up_act = jnp.dot(tokens, up_full, preferred_element_type=jnp.float32)
    tangent_raw = jnp.dot(tokens, vector_full, preferred_element_type=jnp.float32)
    tangent_gate = tangent_raw * inv_root
    gelu_value, gelu_slope, gelu_curve = gelu_parts(pre_gate)
    hidden = (gelu_value * up_act).astype(jnp.bfloat16)
    tangent_hidden = (gelu_slope * tangent_gate * up_act).astype(jnp.bfloat16)
    stacked = jnp.concatenate([hidden, tangent_hidden], axis=0)
    partial_out = lax.dot_general(
        stacked, down_full, (((1,), (1,)), ((), ())), preferred_element_type=jnp.float32
    )
    previous = jnp.concatenate([before_id, segments[:-1]])
    keep_mask = (segments == previous).astype(jnp.float32)[:, None]
    summed = sum_over_shard(partial_out.astype(jnp.bfloat16), 2).astype(jnp.float32)
    grad_out = (keep_mask * (summed[:tok_rows] - target.astype(jnp.float32))).astype(jnp.bfloat16)
    tangent_grad = (keep_mask * summed[tok_rows:]).astype(jnp.bfloat16)
    returned = jnp.concatenate([grad_out, tangent_grad], axis=0)
    back_hidden = jnp.dot(returned, down_full, preferred_element_type=jnp.float32)
    grad_hidden = back_hidden[:tok_rows]
    tangent_grad_hidden = back_hidden[tok_rows:]
    tangent_grad_gate = (
        up_act * (tangent_grad_hidden * gelu_slope + grad_hidden * gelu_curve * tangent_gate)
    ).astype(jnp.bfloat16)

    def own_columns(block):
        cut = block.reshape(tok_rows, 8, 2, depth)
        return lax.dynamic_index_in_dim(cut, core, 2, keepdims=False).reshape(tok_rows, 8 * depth)

    both_tokens = jnp.concatenate([own_columns(tokens), own_columns(other_tokens)], axis=0)
    both_grads = jnp.concatenate([tangent_grad_gate, swapped(tangent_grad_gate)], axis=0)
    partial_curvature = (
        lax.dot_general(
            both_tokens, both_grads, (((0,), (0,)), ((), ())), preferred_element_type=jnp.float32
        )
        * inv_root
    ).astype(jnp.bfloat16)
    return scatter_update(partial_curvature, gradient, vector, 3)


def solution(mesh):
    return jax.shard_map(
        per_device,
        mesh=mesh,
        in_specs=(
            P("dp", None),
            P("dp", None),
            P("dp"),
            P("dp", "shard"),
            P("dp", "shard"),
            P("dp", "shard"),
            P("dp", "shard"),
            P("dp", "shard"),
        ),
        out_specs=P("dp", "shard"),
        check_vma=False,
    )
```

time: 478 us -> 211 us (0.44)
  waiting for transfers between devices: 412 us -> 1.53 us
  Pallas kernels: 0 us -> 168 us
  between operations: 14.9 us -> 1.56 us
  matrix products: 30.2 us -> 17.1 us
  starting transfers between devices: 3.86 us -> 12.8 us
  local copies, waits for them, and re-layouts: 10.6 us -> 4.73 us
    pallas_call x0 -> x3, Pallas kernels: none -> 168 us  [the longest x1 89.8 us: gather(): pl.pallas_call(functools.partial(gather_kernel, count, depth, cut), out_s...]
    psum x1 -> x0, waiting for transfers between devices: 166 us -> none  [per_device(): lax.psum(partial_out.astype(jnp.bfloat16), 'shard').astype(jnp.float32)]
    all_gather x4 -> x0, waiting for transfers between devices: 163 us -> none  [the longest x1 46.2 us: per_device(): lax.all_gather(gate_weight, 'dp', axis=0, tiled=True)]
    reduce_scatter x1 -> x0, waiting for transfers between devices: 80 us -> none  [per_device(): lax.psum_scatter((lax.dot_general(tokens, tangent_grad_gate, (((0,), (0,)...]
    dot_general x4, matrix products: 19.5 us -> 9.83 us  [the longest x1 4.35 us: per_device(): pre_gate = jnp.dot(tokens, gate_full, preferred_element_type=jnp.float32)]
    ppermute x0 -> x2, starting transfers between devices: none -> 7.12 us  [swapped(): return lax.ppermute(block, 'dp', [(i, i ^ 1) for i in range(16)])]
    unnamed x21 -> x22, local copies, waits for them, and re-layouts: 10 us -> 3.39 us
  transfers between devices with their start and end apart: 7 -> 3, of which waited for: 6 -> 1; matrix products, arithmetic and copies ran while one was open for 3% -> 9% of each run, Pallas kernels for 0% -> 70%
where the time goes in v1:
time: 211 us; the launch traced here: 208 us
  Pallas kernels  168 us (80%)
  matrix products  17.1 us (8%)
  starting transfers between devices  12.8 us (6%)
  local copies, waits for them, and re-layouts  4.73 us (2%)
  other arithmetic  2.12 us (1%)
    pallas_call x1, Pallas kernels, gather(): pl.pallas_call(functools.partial(gather_kernel, count, depth, cut), out_s...  89.8 us
    pallas_call x1, Pallas kernels, sum_over_shard(): pl.pallas_call(functools.partial(sum_kernel, rows, width), out_shape=jax....  55.3 us
    pallas_call x1, Pallas kernels, scatter_update(): pl.pallas_call(functools.partial(scatter_kernel, depth, cut, width), out_...  22.8 us
    ppermute x2, starting transfers between devices, swapped(): return lax.ppermute(block, 'dp', [(i, i ^ 1) for i in range(16)])  7.12 us
    ppermute x1, starting transfers between devices, shifted(): return lax.ppermute(block, axis, route)  5.64 us
    dot_general x1, matrix products, per_device(): pre_gate = jnp.dot(tokens, gate_full, preferred_element_type=jnp.float32)  4.35 us
  transfers between devices with their start and end apart: 3, of which 1 were waited for; matrix products, arithmetic and copies ran while one was open for 9% of the time, Pallas kernels for 70%

profile of v1, /device:TPU:1, one launch (start us, length us, event | category | flops | bytes accessed | tf_op | source)
XLA Modules:
  0.0 207.7 jit_solution(5677467234751417439)
XLA Ops:
  0.0 1.3 slice.18
  1.9 5.6 %collective-permute-start.1 = (s32[1]{0:T(128)}, s32[1]{0:T(128)}, u32[]{:S(2)}, u32[]{:S(2)}) collective-permute-start(s32[1]{0:T(128)} %add.34), channel_id=1, source_target_pairs={{0,1},{1,2},{2,3},{3,4},{4,5},{5,6},{6,7},{7,8},{8,9},{9,10},{10,1... | collective-permute-start | bytes 20 | tf_op jit(solution)/shard_map/ppermute | solution.py:430
  7.6 1.6 copy.9
  9.1 0.0 copy-start.3
  9.1 0.1 collective-permute-start
  9.2 89.8 %shard_map.82 = (bf16[2304,1152]{1,0:T(8,128)(2,1)}, bf16[2304,1152]{1,0:T(8,128)(2,1)}, bf16[2304,1152]{1,0:T(8,128)(2,1)}, bf16[2304,1152]{1,0:T(8,128)(2,1)}) custom-call(bf16[144,1152]{1,0:T(8,128)(2,1)} %refs_0_.1, bf16[144,1152]{1,0:T(8,128)(2,1)} %refs_1_.1, bf16[144,1152]{1,0:T(8,128)(2,1)} %v_ref.1, bf16[144,1152]{1,0:T(8,128)(2,1)} %refs_3_.1), custom_call_target="tpu_custom_call" | custom-call | tf_op jit(solution)/shard_map/pallas_call | solution.py:149
  99.1 4.4 %convolution_bitcast_fusion = f32[256,1152]{1,0:T(8,128)S(1)} fusion(bf16[256,2304]{1,0:T(8,128)(2,1)S(1)} %copy-done.3, bf16[2304,1152]{1,0:T(8,128)(2,1)} %get-tuple-element.10), kind=kOutput, calls=%fused_computation.5 | convolution fusion | flops 1358954496 | bytes 7667712 | tf_op jit(solution)/shard_map/dot_general | solution.py:448
  103.5 1.7 fusion.1
  105.2 0.9 slice-done.3
  106.1 2.1 multiply_convert_fusion.1
  108.2 4.0 %convolution_convert_fusion.p_ref = bf16[512,2304]{1,0:T(8,128)(2,1)S(1)} fusion(bf16[2304,1152]{1,0:T(8,128)(2,1)S(1)} %bitcast.25, bf16[256,1152]{1,0:T(8,128)(2,1)S(1)} %get-tuple-element.16, bf16[256,1152]{1,0:T(8,128)(2,1)S(1)} %get-tuple-element.15), kind=kOutput, calls=%fused_computation.2 | convolution fusion | flops 2721447936 | bytes 8847360 | tf_op jit(solution)/shard_map/dot_general | solution.py:456
  112.2 55.3 %shard_map.83 = bf16[512,2304]{1,0:T(8,128)(2,1)S(1)} custom-call(bf16[512,2304]{1,0:T(8,128)(2,1)S(1)} %convolution_convert_fusion.p_ref), custom_call_target="tpu_custom_call" | custom-call | tf_op jit(solution)/shard_map/pallas_call | solution.py:300
  167.5 0.0 copy-start.2
  167.6 0.3 convert_element_type.34
  168.6 0.1 compare_convert_fusion
  168.7 0.2 copy-done.2
  168.8 0.5 fusion.4
  169.3 3.2 %fusion.5 = f32[512,1152]{1,0:T(8,128)S(1)} fusion(bf16[2304,1152]{1,0:T(8,128)(2,1)S(1)} %bitcast.25, bf16[256,2304]{1,0:T(8,128)(2,1)S(1)} %get-tuple-element.14, bf16[256,2304]{1,0:T(8,128)(2,1)S(1)} %get-tuple-element.13), kind=kOutput, calls=%fused_computation.12 | convolution fusion | flops 2722627584 | bytes 10027008 | tf_op jit(solution)/shard_map/dot_general | solution.py:465
  172.5 1.2 fusion.21
  173.8 7.0 %collective-permute-start.2 = (bf16[256,1152]{1,0:T(8,128)(2,1)S(1)}, bf16[256,1152]{1,0:T(8,128)(2,1)S(1)}, u32[]{:S(2)}, u32[]{:S(2)}) collective-permute-start(bf16[256,1152]{1,0:T(8,128)(2,1)S(1)} %fusion.21), channel_id=1, source_target_pairs={{0,1},{1,0},{2,3},{3,2},{4,5},{5,4},{6,7},{7,6},{8,9},{9,8},{10,11... | collective-permute-start | bytes 1769480 | tf_op jit(solution)/shard_map/ppermute | solution.py:434
  180.9 1.5 collective-permute-done.2
  182.4 1.7 fusion.p_ref
  184.1 22.8 %shard_map.84 = bf16[144,1152]{1,0:T(8,128)(2,1)S(1)} custom-call(bf16[1152,1152]{1,0:T(8,128)(2,1)S(1)} %fusion.p_ref, bf16[144,1152]{1,0:T(8,128)(2,1)S(1)} %copy-done.1, bf16[144,1152]{1,0:T(8,128)(2,1)S(1)} %copy-done), custom_call_target="tpu_custom_call" | custom-call | tf_op jit(solution)/shard_map/pallas_call | solution.py:410
  206.9 0.7 copy.12
  (22 shorter events, 0.1 us)
Async XLA Ops:
  1.9 166.0 %collective-permute-start.1 = (s32[1]{0:T(128)}, s32[1]{0:T(128)}, u32[]{:S(2)}, u32[]{:S(2)}) collective-permute-start(s32[1]{0:T(128)} %add.34), channel_id=1, source_target_pairs={{0,1},{1,2},{2,3},{3,4},{4,5},{5,6},{6,7},{7,8},{8,9},{9,10},{10,1... | collective-permute-start | bytes 20 | tf_op jit(solution)/shard_map/ppermute | solution.py:430
  9.1 89.9 %copy-start.3 = (bf16[256,2304]{1,0:T(8,128)(2,1)S(1)}, bf16[256,2304]{1,0:T(8,128)(2,1)}, u32[]{:S(2)}) copy-start(bf16[256,2304]{1,0:T(8,128)(2,1)} %param.8) | copy-start | bytes 3538948
  9.1 171.7 %collective-permute-start = (bf16[256,2304]{0,1:T(8,128)(2,1)S(1)}, bf16[256,2304]{0,1:T(8,128)(2,1)S(1)}, u32[]{:S(2)}, u32[]{:S(2)}) collective-permute-start(bf16[256,2304]{0,1:T(8,128)(2,1)S(1)} %copy.9), channel_id=1, source_target_pairs={{0,1},{1,0},{2,3},{3,2},{4,5},{5,4},{6,7},{7,6},{8,9},{9,8},{10,11... | collective-permute-start | bytes 3538952 | tf_op jit(solution)/shard_map/ppermute | solution.py:434
  99.1 4.4 %copy-start.5 = (bf16[2304,1152]{1,0:T(8,128)(2,1)S(1)}, bf16[2304,1152]{1,0:T(8,128)(2,1)}, u32[]{:S(2)}) copy-start(bf16[2304,1152]{1,0:T(8,128)(2,1)} %get-tuple-element.11) | copy-start | bytes 15925252
  99.1 6.1 %slice-start.2 = ((s8[5308416]{0:T(1024)(128)(4,1)}), s8[4194304]{0:T(1024)(128)(4,1)S(1)}, s32[]{:S(2)}) async-start(s8[5308416]{0:T(1024)(128)(4,1)} %bitcast.26), calls=%async_computation.2 | async-start | bytes 8388608
  99.1 9.1 %slice-start = ((s8[5308416]{0:T(1024)(128)(4,1)}), s8[4194304]{0:T(1024)(128)(4,1)S(1)}, s32[]{:S(2)}) async-start(s8[5308416]{0:T(1024)(128)(4,1)} %bitcast.24), calls=%async_computation | async-start | bytes 8388608
  103.5 2.6 %slice-start.3 = ((s8[5308416]{0:T(1024)(128)(4,1)}), s8[1114112]{0:T(1024)(128)(4,1)S(1)}, s32[]{:S(2)}) async-start(s8[5308416]{0:T(1024)(128)(4,1)} %bitcast.26), calls=%async_computation.3 | async-start | bytes 2228224
  103.5 4.7 %slice-start.1 = ((s8[5308416]{0:T(1024)(128)(4,1)}), s8[1114112]{0:T(1024)(128)(4,1)S(1)}, s32[]{:S(2)}) async-start(s8[5308416]{0:T(1024)(128)(4,1)} %bitcast.24), calls=%async_computation.1 | async-start | bytes 2228224
  167.5 1.0 copy-start.4
  167.5 1.3 copy-start.2
  173.8 8.7 %collective-permute-start.2 = (bf16[256,1152]{1,0:T(8,128)(2,1)S(1)}, bf16[256,1152]{1,0:T(8,128)(2,1)S(1)}, u32[]{:S(2)}, u32[]{:S(2)}) collective-permute-start(bf16[256,1152]{1,0:T(8,128)(2,1)S(1)} %fusion.21), channel_id=1, source_target_pairs={{0,1},{1,0},{2,3},{3,2},{4,5},{5,4},{6,7},{7,6},{8,9},{9,8},{10,11... | collective-permute-start | bytes 1769480 | tf_op jit(solution)/shard_map/ppermute | solution.py:434
  182.4 1.7 copy-start
  182.4 1.7 copy-start.1

commit v2 on v0

v2 whole, which is shorter than its diff:
```python
import functools

import jax
import jax.numpy as jnp
from jax import lax
from jax.experimental import pallas as pl
from jax.experimental.pallas import tpu as pltpu
from jax.sharding import PartitionSpec as P

MESH = pl.DeviceIdType.MESH
coeff_k = 0.7978845608028654
coeff_c = 0.044715
damping = 0.01
step_size = 0.8


def gelu_parts(pre_act):
    inner_arg = coeff_k * (pre_act + coeff_c * pre_act * pre_act * pre_act)
    tanh_value = jnp.tanh(inner_arg)
    slope_term = coeff_k * (1.0 + 3.0 * coeff_c * pre_act * pre_act)
    curve_term = 6.0 * coeff_k * coeff_c * pre_act
    sech_square = 1.0 - tanh_value * tanh_value
    gelu_value = 0.5 * pre_act * (1.0 + tanh_value)
    gelu_slope = 0.5 * (1.0 + tanh_value) + 0.5 * pre_act * sech_square * slope_term
    gelu_curve = sech_square * (
        slope_term + 0.5 * pre_act * (curve_term - 2.0 * tanh_value * slope_term * slope_term)
    )
    return (gelu_value, gelu_slope, gelu_curve)


def remote(src, dst, send_sem, recv_sem, axis, index):
    return pltpu.make_async_remote_copy(
        src_ref=src,
        dst_ref=dst,
        send_sem=send_sem,
        recv_sem=recv_sem,
        device_id={axis: index},
        device_id_type=MESH,
    )


GATHER_COPIES = 17
PARTS = 3


def plus(a, *more):
    total = a.astype(jnp.float32)
    for b in more:
        total = total + b.astype(jnp.float32)
    return total


def dot_nn(a, b):
    return jnp.dot(a, b, preferred_element_type=jnp.float32)


def dot_nt(a, b):
    return lax.dot_general(a, b, (((1,), (1,)), ((), ())), preferred_element_type=jnp.float32)


def dot_tn(a, b):
    return lax.dot_general(a, b, (((0,), (0,)), ((), ())), preferred_element_type=jnp.float32)


def step_kernel(
    dims, tok_hbm, tgt_hbm, seg_hbm, gate_hbm, up_hbm, vec_hbm, down_hbm, grad_hbm, o_ref,
    full, tok, tgt, tok4, tok_t, tok_t2, tgt_t, seg, seg_prev, keep, acc, stacked, p, back, gt,
    xin, xtx, xc, zin, ztx, tgg, tgg2, cp, cin, cout, grad,
    gs, gr, sx, rx, sz, rz, s4, r4, cs, cr, ms, mr, ls,
):
    tok_rows, width, depth, cols = dims
    bf = jnp.bfloat16
    d, sh = lax.axis_index("dp"), lax.axis_index("shard")
    y, zl, core = d // 4, (d // 2) % 2, d % 2
    x, zh = sh % 4, sh // 4
    piece = 4 * depth
    cut = (depth // 32 + 1) * 16
    part = cols // PARTS
    inv_root = float(width) ** (-0.5)

    def at(dy, dz, dc):
        return ((y + dy) % 4) * 4 + ((zl + dz) % 2) * 2 + (core + dc) % 2

    sib, up, down, zed = at(0, 0, 1), at(1, 0, 0), at(-1, 0, 0), at(0, 1, 0)
    right, left = zh * 4 + (x + 1) % 4, zh * 4 + (x + 3) % 4
    above, below = ((zh + 1) % 4) * 4 + x, ((zh + 3) % 4) * 4 + x
    after, before = (d + 1) % 16, (d + 15) % 16
    barrier = pltpu.get_barrier_semaphore()
    for axis, targets in (("dp", (sib, up, down, zed, after, before)), ("shard", (right, left, above, below))):
        for t in targets:
            pl.semaphore_signal(barrier, inc=1, device_id={axis: t}, device_id_type=MESH)

    loads = [
        pltpu.make_async_copy(src, dst, ls.at[i])
        for i, (src, dst) in enumerate(((tok_hbm, tok), (tgt_hbm, tgt), (seg_hbm, seg), (grad_hbm, grad)))
    ]
    for copy in loads:
        copy.start()
    pl.semaphore_wait(barrier, 10)

    sent = []

    def go(src, dst, s, r, axis, target):
        copy = remote(src, dst, s, r, axis, target)
        copy.start()
        sent.append(copy)

    def got(ref, s, r):
        remote(ref, ref, s, r, "dp", sib).wait_recv()

    def rows(w, owner, which):
        lo, size = {"w": (0, depth), "a": (0, cut), "b": (cut, depth - cut)}[which]
        return full.at[w, pl.ds(pl.multiple_of(owner * depth + lo, 16), size)]

    me = at(0, 0, 0)
    table = [
        (me, "w", sib, at(0, 0, 1)),
        (me, "w", up, at(-1, 0, 0)),
        (me, "w", down, at(1, 0, 0)),
        (me, "w", zed, at(0, 1, 0)),
        (at(0, 1, 0), "w", up, at(-1, 1, 0)),
        (at(0, 1, 0), "w", down, at(1, 1, 0)),
        (at(0, 1, 0), "w", sib, at(0, 1, 1)),
        (at(-1, 0, 0), "a", up, at(2, 0, 0)),
        (at(1, 0, 0), "b", down, at(2, 0, 0)),
        (at(-1, 0, 0), "w", sib, at(-1, 0, 1)),
        (at(1, 0, 0), "w", sib, at(1, 0, 1)),
        (at(-1, 1, 0), "w", sib, at(-1, 1, 1)),
        (at(1, 1, 0), "w", sib, at(1, 1, 1)),
        (at(2, 0, 0), "a", zed, at(2, 1, 0)),
        (at(2, 0, 0), "b", zed, at(2, 1, 0)),
        (at(2, 0, 0), "w", sib, at(2, 0, 1)),
        (at(2, 1, 0), "w", sib, at(2, 1, 1)),
    ]
    ins = (gate_hbm, up_hbm, vec_hbm, down_hbm)

    def start(w, *numbers):
        for k in numbers:
            owner, which, target, _ = table[k]
            src = ins[w] if k < 4 else rows(w, owner, which)
            go(src, rows(w, owner, which), gs.at[w, k], gr.at[w, k], "dp", target)

    def wait(w, *numbers):
        for k in numbers:
            _, which, _, owner = table[k]
            got(rows(w, owner, which), gs.at[w, k], gr.at[w, k])

    own_copies = [pltpu.make_async_copy(ins[w], rows(w, me, "w"), ls.at[4 + w]) for w in range(4)]

    def stage_a(w):
        wait(w, 3)
        start(w, 4, 5, 6)
        wait(w, 1)
        start(w, 7, 9)
        wait(w, 2)
        start(w, 8, 10)

    def stage_b(w):
        wait(w, 7)
        start(w, 13)
        wait(w, 8)
        start(w, 14, 15)
        wait(w, 4)
        start(w, 11)
        wait(w, 5)
        start(w, 12)

    def stage_c(w):
        wait(w, 13, 14)
        start(w, 16)

    late = {0: (0, 6), -1: (9, 11), 1: (10, 12), 2: (15, 16)}

    def piece_of(rel):
        return (y + rel) % 4

    def piece_rows(rel):
        return pl.ds(pl.multiple_of(piece_of(rel) * piece, 16), piece)

    def use(w, rel):
        wait(w, *late[rel])
        if rel == 0:
            own_copies[w].wait()

        def chunk(n, _):
            c = pl.ds(pl.multiple_of(n * 384, 128), 384)
            term = dot_nn(tok4[piece_of(rel)], full[w, piece_rows(rel), c])
            if rel == 0:
                acc[w, :, c] = term
            else:
                acc[w, :, c] += term
            return 0

        lax.fori_loop(0, cols // 384, chunk, 0)

    start(0, 1, 2, 3, 0)
    own_copies[0].start()
    go(seg_hbm, seg_prev, ms.at[0], mr.at[0], "dp", after)
    start(1, 1, 2, 3, 0)
    own_copies[1].start()

    loads[0].wait()
    for r in range(4):
        tok4[r] = tok[:, r * piece : (r + 1) * piece]

    def turn(src, dst):
        def body(j, _):
            c = pl.ds(pl.multiple_of(j * 128, 128), 128)
            dst[c, :] = src[:, c].astype(jnp.float32).T.astype(bf)
            return 0

        lax.fori_loop(0, width // 128, body, 0)

    turn(tok, tok_t)
    go(tok_t, tok_t2, ms.at[1], mr.at[1], "dp", sib)
    loads[1].wait()
    turn(tgt, tgt_t)

    stage_a(0)
    start(2, 1, 2, 3, 0)
    own_copies[2].start()
    stage_a(1)
    stage_b(0)
    use(0, 0)
    stage_a(2)
    start(3, 1, 2)
    own_copies[3].start()
    stage_b(1)
    use(1, 0)
    stage_c(0)
    use(0, -1)
    use(0, 1)
    stage_b(2)
    start(3, 3, 0)
    use(2, 0)
    stage_c(1)
    use(1, -1)
    use(1, 1)
    use(0, 2)
    use(2, -1)
    use(2, 1)
    use(1, 2)
    stage_c(2)
    stage_a(3)
    use(2, 2)

    loads[2].wait()
    got(seg_prev, ms.at[0], mr.at[0])
    lane = lax.broadcasted_iota(jnp.int32, (8, tok_rows), 1)
    here = jnp.broadcast_to(seg[...], (8, tok_rows))
    previous = jnp.where(
        lane == 0,
        pltpu.roll(jnp.broadcast_to(seg_prev[...], (8, tok_rows)), 1, 1),
        pltpu.roll(here, 1, 1),
    )
    first = (lane + d) == 0
    keep[...] = jnp.where(first, 0.0, jnp.where(here == previous, 1.0, 0.0))

    def pointwise(i, _):
        r = pl.ds(pl.multiple_of(i * 16, 16), 16)
        r2 = pl.ds(pl.multiple_of(tok_rows + i * 16, 16), 16)
        value, slope, curve = gelu_parts(acc[0, r])
        up_act = acc[1, r]
        tangent = acc[2, r] * inv_root
        stacked[r] = (value * up_act).astype(bf)
        stacked[r2] = (slope * tangent * up_act).astype(bf)
        acc[0, r] = up_act * slope
        acc[1, r] = up_act * curve * tangent
        return 0

    lax.fori_loop(0, tok_rows // 16, pointwise, 0)

    order = (0, -1, 1, 2)

    def out_piece(rel):
        wait(3, *late[rel])
        if rel == 0:
            own_copies[3].wait()

        def chunk(n, _):
            r = pl.ds(pl.multiple_of(piece_of(rel) * piece + n * depth, 16), depth)
            p[r] = dot_nt(full[3, r], stacked[...]).astype(bf)
            return 0

        lax.fori_loop(0, 4, chunk, 0)

    def x_src(q):
        def src(chunk, lo, size):
            r = pl.ds(pl.multiple_of(piece_of(order[q]) * piece + lo, 16), size)
            return p.at[r, pl.ds(pl.multiple_of(((x + chunk) % 4) * 128, 128), 128)]

        return src

    def z_src(q):
        def src(chunk, lo, size):
            return xc.at[q, pl.ds(pl.multiple_of(((zh + chunk) % 4) * depth + lo, 16), size)]

        return src

    def ring1(q, src, size, mid, inbox, s, r, plus1, minus1):
        rest = size - mid
        for i, (dst, frm, lo, n, target) in enumerate((
            (0, 2, mid, rest, plus1), (0, 2, 0, mid, minus1), (1, 1, 0, mid, plus1), (2, 3, mid, rest, minus1),
        )):
            go(src(frm, lo, n), inbox.at[q, dst, pl.ds(lo, n)], s.at[q, i], r.at[q, i], "shard", target)

    def ring2(q, src, size, mid, inbox, out, s, r, plus1, minus1):
        rest = size - mid
        for i, (dst, frm, lo, n, target) in enumerate(((1, 1, mid, rest, plus1), (2, 3, 0, mid, minus1))):
            came = inbox.at[q, 0, pl.ds(lo, n)]
            got(came, s.at[q, i], r.at[q, i])
            out[q, lo : lo + n] = plus(src(frm, lo, n)[...], came[...]).astype(bf)
            go(out.at[q, pl.ds(lo, n)], inbox.at[q, dst, pl.ds(lo, n)], s.at[q, 4 + i], r.at[q, 4 + i], "shard", target)

    def ring3(q, src, size, mid, inbox, s, r):
        got(inbox.at[q, 1, pl.ds(0, mid)], s.at[q, 2], r.at[q, 2])
        got(inbox.at[q, 2, pl.ds(mid, size - mid)], s.at[q, 3], r.at[q, 3])
        got(inbox.at[q, 1, pl.ds(mid, size - mid)], s.at[q, 4], r.at[q, 4])
        got(inbox.at[q, 2, pl.ds(0, mid)], s.at[q, 5], r.at[q, 5])
        return plus(src(0, 0, size)[...], inbox[q, 1], inbox[q, 2])

    def g_block(q, lo, size, chunk):
        r = pl.ds(pl.multiple_of(piece_of(order[q]) * piece + lo, 16), size)
        return gt.at[r, pl.ds(pl.multiple_of(((x + chunk) % 4) * 128, 128), 128)]

    def send_g(q, i, ref, target):
        go(ref, ref, s4.at[q, i], r4.at[q, i], "shard", target)

    def got_g(q, i, ref):
        got(ref, s4.at[q, i], r4.at[q, i])

    def step(i, q):
        half = piece // 2
        if i == 0:
            ring1(q, x_src(q), piece, half, xin, sx, rx, right, left)
        if i == 1:
            ring2(q, x_src(q), piece, half, xin, xtx, sx, rx, right, left)
        if i == 2:
            xc[q] = ring3(q, x_src(q), piece, half, xin, sx, rx).astype(bf)
            ring1(q, z_src(q), depth, cut, zin, sz, rz, above, below)
        if i == 3:
            ring2(q, z_src(q), depth, cut, zin, ztx, sz, rz, above, below)
        if i == 4:
            total = ring3(q, z_src(q), depth, cut, zin, sz, rz)
            lanes = pl.ds(pl.multiple_of((x % 2) * 128, 128), 128)
            r = pl.ds(pl.multiple_of(piece_of(order[q]) * piece + zh * depth, 16), depth)
            is_out = (1 - x // 2).astype(jnp.float32)
            wanted = tgt_t[r, lanes].astype(jnp.float32) * is_out
            mine = g_block(q, zh * depth, depth, 0)
            mine[...] = (keep[0:1, lanes] * (total - wanted)).astype(bf)
            send_g(q, 0, mine, above)
            send_g(q, 1, mine, below)
        if i == 5:
            lo, hi = ((zh + 3) % 4) * depth, ((zh + 1) % 4) * depth
            got_g(q, 0, g_block(q, lo, depth, 0))
            send_g(q, 2, g_block(q, lo, cut, 0), above)
            got_g(q, 1, g_block(q, hi, depth, 0))
            send_g(q, 3, g_block(q, hi + cut, depth - cut, 0), below)
        if i == 6:
            far = ((zh + 2) % 4) * depth
            got_g(q, 2, g_block(q, far, cut, 0))
            got_g(q, 3, g_block(q, far + cut, depth - cut, 0))
            send_g(q, 4, g_block(q, 0, piece, 0), right)
            send_g(q, 5, g_block(q, 0, piece, 0), left)
        if i == 7:
            got_g(q, 4, g_block(q, 0, piece, 3))
            send_g(q, 6, g_block(q, 0, half, 3), right)
            got_g(q, 5, g_block(q, 0, piece, 1))
            send_g(q, 7, g_block(q, half, half, 1), left)
        if i == 8:
            got_g(q, 6, g_block(q, 0, half, 2))
            got_g(q, 7, g_block(q, half, half, 2))

            def chunk(n, _):
                c = pl.ds(pl.multiple_of(n * 384, 128), 384)
                term = dot_tn(gt[piece_rows(order[q])], full[3, piece_rows(order[q]), c])
                if q == 0:
                    back[:, c] = term
                else:
                    back[:, c] += term
                return 0

            lax.fori_loop(0, cols // 384, chunk, 0)

    out_piece(0)
    step(0, 0)
    stage_b(3)
    out_piece(-1)
    step(0, 1)
    step(1, 0)
    out_piece(1)
    step(0, 2)
    step(1, 1)
    step(2, 0)
    stage_c(3)
    step(3, 0)
    step(2, 1)
    step(1, 2)
    out_piece(2)
    step(0, 3)
    for t in range(4, 12):
        for q in range(4):
            i = t - q
            if 0 <= i < 9:
                step(i, q)

    loads[3].wait()
    got(tok_t2, ms.at[1], mr.at[1])

    def pc(q):
        return pl.ds(q * part, part)

    def chip(dy, dz):
        return at(dy, dz, 0) // 2

    def c_block(dy, dz, q, lo=0, size=depth):
        return cp.at[pl.ds(pl.multiple_of(chip(dy, dz) * depth + lo, 16), size), pc(q)]

    def make(q, *which):
        for dy, dz in which:
            r = pl.ds(pl.multiple_of(at(dy, dz, 0) * depth, 16), depth)
            total = dot_nn(tok_t[r], tgg[:, pc(q)]) + dot_nn(tok_t2[r], tgg2[:, pc(q)])
            c_block(dy, dz, q)[...] = (total * inv_root).astype(bf)

    def box(slot, q, lo=0, size=depth):
        return cin.at[slot, pl.ds(lo, size), pc(q)]

    def send_c(src, dst, k, q, target):
        go(src, dst, cs.at[q, k], cr.at[q, k], "dp", target)

    def got_c(ref, k, q):
        got(ref, cs.at[q, k], cr.at[q, k])

    rest = depth - cut

    def reduce_step(i, q):
        if i == 0:
            got(tgg2.at[:, pc(q)], ms.at[2 + q], mr.at[2 + q])
            make(q, (2, 1), (1, 1), (-1, 1))
            send_c(c_block(2, 1, q), box(0, q), 0, q, zed)
            send_c(c_block(1, 1, q), box(1, q), 1, q, up)
            send_c(c_block(-1, 1, q), box(2, q), 2, q, down)
            make(q, (2, 0), (0, 1), (1, 0), (-1, 0), (0, 0))
        if i == 1:
            got_c(box(0, q), 0, q)
            cout[0, :, pc(q)] = plus(c_block(2, 0, q)[...], box(0, q)[...]).astype(bf)
            send_c(cout.at[0, pl.ds(0, cut), pc(q)], box(3, q, 0, cut), 3, q, up)
            send_c(cout.at[0, pl.ds(cut, rest), pc(q)], box(3, q, cut, rest), 4, q, down)
            got_c(box(1, q), 1, q)
            got_c(box(2, q), 2, q)
            cout[1, :, pc(q)] = plus(c_block(0, 1, q)[...], box(1, q)[...], box(2, q)[...]).astype(bf)
            send_c(cout.at[1, :, pc(q)], box(4, q), 5, q, zed)
        if i == 2:
            got_c(box(3, q, 0, cut), 3, q)
            cout[2, :cut, pc(q)] = plus(c_block(1, 0, q, 0, cut)[...], box(3, q, 0, cut)[...]).astype(bf)
            cout[2, cut:, pc(q)] = c_block(1, 0, q, cut, rest)[...]
            send_c(cout.at[2, :, pc(q)], box(5, q), 6, q, up)
            got_c(box(3, q, cut, rest), 4, q)
            cout[3, cut:, pc(q)] = plus(c_block(-1, 0, q, cut, rest)[...], box(3, q, cut, rest)[...]).astype(bf)
            cout[3, :cut, pc(q)] = c_block(-1, 0, q, 0, cut)[...]
            send_c(cout.at[3, :, pc(q)], box(6, q), 7, q, down)
        if i == 3:
            got_c(box(4, q), 5, q)
            got_c(box(5, q), 6, q)
            got_c(box(6, q), 7, q)
            total = plus(c_block(0, 0, q)[...], box(4, q)[...], box(5, q)[...], box(6, q)[...])
            own = full[2, pl.ds(pl.multiple_of(me * depth, 16), depth), pc(q)]
            o_ref[:, pc(q)] = (
                grad[:, pc(q)].astype(jnp.float32)
                + (1.0 - damping) * own.astype(jnp.float32)
                - step_size * total
            ).astype(bf)

    for q in range(PARTS):

        def combine(i, _):
            r = pl.ds(pl.multiple_of(i * 32, 16), 32)
            r2 = pl.ds(pl.multiple_of(tok_rows + i * 32, 16), 32)
            tgg[r, pc(q)] = (acc[0, r, pc(q)] * back[r2, pc(q)] + acc[1, r, pc(q)] * back[r, pc(q)]).astype(bf)
            return 0

        lax.fori_loop(0, tok_rows // 32, combine, 0)
        go(tgg.at[:, pc(q)], tgg2.at[:, pc(q)], ms.at[2 + q], mr.at[2 + q], "dp", sib)
    for t in range(4 + PARTS - 1):
        for q in range(PARTS):
            if 0 <= t - q < 4:
                reduce_step(t - q, q)
    for copy in sent:
        copy.wait_send()


def per_device(tokens, target, segments, gate_weight, up_weight, down_weight, vector, gradient):
    tok_rows, width = tokens.shape
    depth, cols = gate_weight.shape
    bf, f32 = jnp.bfloat16, jnp.float32
    piece = 4 * depth
    cut = (depth // 32 + 1) * 16
    vm, dma = pltpu.VMEM, pltpu.SemaphoreType.DMA
    anywhere = pl.BlockSpec(memory_space=pl.ANY)
    scratch = [
        vm((4, width, cols), bf),
        vm((tok_rows, width), bf),
        vm((tok_rows, width), bf),
        vm((4, tok_rows, piece), bf),
        vm((width, tok_rows), bf),
        vm((width, tok_rows), bf),
        vm((width, tok_rows), bf),
        vm((1, tok_rows), jnp.int32),
        vm((1, tok_rows), jnp.int32),
        vm((8, tok_rows), f32),
        vm((3, tok_rows, cols), f32),
        vm((2 * tok_rows, cols), bf),
        vm((width, 2 * tok_rows), bf),
        vm((2 * tok_rows, cols), f32),
        vm((width, 2 * tok_rows), bf),
        vm((4, 3, piece, 128), bf),
        vm((4, piece, 128), bf),
        vm((4, piece, 128), bf),
        vm((4, 3, depth, 128), bf),
        vm((4, depth, 128), bf),
        vm((tok_rows, cols), bf),
        vm((tok_rows, cols), bf),
        vm((8 * depth, cols), bf),
        vm((7, depth, cols), bf),
        vm((4, depth, cols), bf),
        vm((depth, cols), bf),
        dma((4, GATHER_COPIES)),
        dma((4, GATHER_COPIES)),
        dma((4, 6)),
        dma((4, 6)),
        dma((4, 6)),
        dma((4, 6)),
        dma((4, 8)),
        dma((4, 8)),
        dma((PARTS, 8)),
        dma((PARTS, 8)),
        dma((2 + PARTS,)),
        dma((2 + PARTS,)),
        dma((8,)),
    ]
    return pl.pallas_call(
        functools.partial(step_kernel, (tok_rows, width, depth, cols)),
        out_shape=jax.ShapeDtypeStruct((depth, cols), bf),
        in_specs=[anywhere] * 8,
        out_specs=pl.BlockSpec(memory_space=pltpu.VMEM),
        scratch_shapes=scratch,
        compiler_params=pltpu.CompilerParams(
            collective_id=1, has_side_effects=True, vmem_limit_bytes=62 * 2**20
        ),
    )(tokens, target, segments[None], gate_weight, up_weight, vector, down_weight, gradient)


def solution(mesh):
    return jax.shard_map(
        per_device,
        mesh=mesh,
        in_specs=(
            P("dp", None),
            P("dp", None),
            P("dp"),
            P("dp", "shard"),
            P("dp", "shard"),
            P("dp", "shard"),
            P("dp", "shard"),
            P("dp", "shard"),
        ),
        out_specs=P("dp", "shard"),
        check_vma=False,
    )
```

time: 478 us -> 182 us (0.38)
  waiting for transfers between devices: 412 us -> 0 us
  Pallas kernels: 0 us -> 178 us
  matrix products: 30.2 us -> 0 us
  between operations: 14.9 us -> 0.01 us
  local copies, waits for them, and re-layouts: 10.6 us -> 1.73 us
    pallas_call x0 -> x1, Pallas kernels: none -> 178 us  [per_device(): pl.pallas_call(functools.partial(step_kernel, (tok_rows, width, depth, co...]
    psum x1 -> x0, waiting for transfers between devices: 166 us -> none  [per_device(): lax.psum(partial_out.astype(jnp.bfloat16), 'shard').astype(jnp.float32)]
    all_gather x4 -> x0, waiting for transfers between devices: 163 us -> none  [the longest x1 46.2 us: per_device(): lax.all_gather(gate_weight, 'dp', axis=0, tiled=True)]
    reduce_scatter x1 -> x0, waiting for transfers between devices: 80 us -> none  [per_device(): lax.psum_scatter((lax.dot_general(tokens, tangent_grad_gate, (((0,), (0,)...]
    dot_general x6 -> x0, matrix products: 30.2 us -> none  [the longest x1 7.52 us: per_device(): lax.dot_general(stacked, down_full, (((1,), (1,)), ((), ())), preferred_e...]
    unnamed x21 -> x1, local copies, waits for them, and re-layouts: 10 us -> 1.73 us
  transfers between devices with their start and end apart: 7 -> 0, of which waited for: 6 -> 0; matrix products, arithmetic and copies ran while one was open for 3% -> 0% of each run, Pallas kernels for 0% -> 0%
where the time goes in v2:
time: 182 us; the launch traced here: 180 us
  Pallas kernels  178 us (98%)
    pallas_call x1, Pallas kernels, per_device(): pl.pallas_call(functools.partial(step_kernel, (tok_rows, width, depth, co...  178 us

profile of v2, /device:TPU:1, one launch (start us, length us, event | category | flops | bytes accessed | tf_op | source)
XLA Modules:
  0.0 180.0 jit_solution(16294570983582660955)
XLA Ops:
  0.0 178.2 %shard_map.82 = bf16[144,1152]{1,0:T(8,128)(2,1)} custom-call(bf16[256,2304]{1,0:T(8,128)(2,1)} %tok_hbm.1, bf16[256,2304]{1,0:T(8,128)(2,1)} %tgt_hbm.1, s32[1,256]{1,0:T(1,128)} %bitcast.1, bf16[144,1152]{1,0:T(8,128)(2,1)} %gate_hbm.1, bf16[144,1152]{1,0:T(8,128)(2,1)} %up_hbm.1, bf16[144,1152]{1,0:T(8,128)(2,1)} %vec_hbm.1, bf16[144,1152]{1,0:T(8,128)(2,1)} %down_hbm.1, ...), custom_call_target="tpu_custom_call" | custom-call | tf_op jit(solution)/shard_map/pallas_call | solution.py:541
  178.2 1.7 copy.10

commit v3 on v2

--- a/solution.py
+++ b/solution.py
@@ -39,7 +39,7 @@
     )
 
 
-GATHER_COPIES = 17
+GATHER_COPIES = 19
 PARTS = 3
 
 
@@ -65,7 +65,7 @@
 def step_kernel(
     dims, tok_hbm, tgt_hbm, seg_hbm, gate_hbm, up_hbm, vec_hbm, down_hbm, grad_hbm, o_ref,
     full, tok, tgt, tok4, tok_t, tok_t2, tgt_t, seg, seg_prev, keep, acc, stacked, p, back, gt,
-    xin, xtx, xc, zin, ztx, tgg, tgg2, cp, cin, cout, grad,
+    xin, xtx, xc, zin, tgg, tgg2, cp, cin, cout, grad,
     gs, gr, sx, rx, sz, rz, s4, r4, cs, cr, ms, mr, ls,
 ):
     tok_rows, width, depth, cols = dims
@@ -84,9 +84,10 @@
     sib, up, down, zed = at(0, 0, 1), at(1, 0, 0), at(-1, 0, 0), at(0, 1, 0)
     right, left = zh * 4 + (x + 1) % 4, zh * 4 + (x + 3) % 4
     above, below = ((zh + 1) % 4) * 4 + x, ((zh + 3) % 4) * 4 + x
+    across = ((zh + 2) % 4) * 4 + x
     after, before = (d + 1) % 16, (d + 15) % 16
     barrier = pltpu.get_barrier_semaphore()
-    for axis, targets in (("dp", (sib, up, down, zed, after, before)), ("shard", (right, left, above, below))):
+    for axis, targets in (("dp", (sib, up, down, zed, after, before)), ("shard", (right, left, above, below, across))):
         for t in targets:
             pl.semaphore_signal(barrier, inc=1, device_id={axis: t}, device_id_type=MESH)
 
@@ -96,7 +97,7 @@
     ]
     for copy in loads:
         copy.start()
-    pl.semaphore_wait(barrier, 10)
+    pl.semaphore_wait(barrier, 11)
 
     sent = []
 
@@ -108,66 +109,60 @@
     def got(ref, s, r):
         remote(ref, ref, s, r, "dp", sib).wait_recv()
 
-    def rows(w, owner, which):
+    def place(dy, dz, dc):
+        return {0: 2 * dz, -1: 4 + 4 * dz, 1: 6 + 4 * dz, 2: 12 + 2 * dz}[dy] + dc
+
+    def rows(w, rel, which):
         lo, size = {"w": (0, depth), "a": (0, cut), "b": (cut, depth - cut)}[which]
-        return full.at[w, pl.ds(pl.multiple_of(owner * depth + lo, 16), size)]
+        base = place(*rel) if w == 3 else at(*rel)
+        return full.at[w, pl.ds(pl.multiple_of(base * depth + lo, 16), size)]
 
     me = at(0, 0, 0)
     table = [
-        (me, "w", sib, at(0, 0, 1)),
-        (me, "w", up, at(-1, 0, 0)),
-        (me, "w", down, at(1, 0, 0)),
-        (me, "w", zed, at(0, 1, 0)),
-        (at(0, 1, 0), "w", up, at(-1, 1, 0)),
-        (at(0, 1, 0), "w", down, at(1, 1, 0)),
-        (at(0, 1, 0), "w", sib, at(0, 1, 1)),
-        (at(-1, 0, 0), "a", up, at(2, 0, 0)),
-        (at(1, 0, 0), "b", down, at(2, 0, 0)),
-        (at(-1, 0, 0), "w", sib, at(-1, 0, 1)),
-        (at(1, 0, 0), "w", sib, at(1, 0, 1)),
-        (at(-1, 1, 0), "w", sib, at(-1, 1, 1)),
-        (at(1, 1, 0), "w", sib, at(1, 1, 1)),
-        (at(2, 0, 0), "a", zed, at(2, 1, 0)),
-        (at(2, 0, 0), "b", zed, at(2, 1, 0)),
-        (at(2, 0, 0), "w", sib, at(2, 0, 1)),
-        (at(2, 1, 0), "w", sib, at(2, 1, 1)),
+        ((0, 0, 0), "w", sib, (0, 0, 1)),
+        ((0, 0, 0), "w", up, (-1, 0, 0)),
+        ((0, 0, 0), "w", down, (1, 0, 0)),
+        ((0, 0, 0), "w", zed, (0, 1, 0)),
+        ((0, 1, 0), "w", up, (-1, 1, 0)),
+        ((0, 1, 0), "w", down, (1, 1, 0)),
+        ((0, 1, 0), "w", sib, (0, 1, 1)),
+        ((-1, 0, 0), "a", up, (2, 0, 0)),
+        ((1, 0, 0), "b", down, (2, 0, 0)),
+        ((-1, 0, 0), "w", sib, (-1, 0, 1)),
+        ((1, 0, 0), "w", sib, (1, 0, 1)),
+        ((-1, 1, 0), "w", sib, (-1, 1, 1)),
+        ((1, 1, 0), "w", sib, (1, 1, 1)),
+        ((2, 0, 0), "a", zed, (2, 1, 0)),
+        ((2, 0, 0), "b", zed, (2, 1, 0)),
+        ((2, 0, 0), "w", sib, (2, 0, 1)),
+        ((2, 1, 0), "w", sib, (2, 1, 1)),
     ]
+    halves = {
+        1: ((0, 0, 0), "a", up, (-1, 0, 0)),
+        2: ((0, 0, 0), "b", down, (1, 0, 0)),
+        17: ((0, 0, 0), "b", up, (-1, 0, 0)),
+        18: ((0, 0, 0), "a", down, (1, 0, 0)),
+    }
     ins = (gate_hbm, up_hbm, vec_hbm, down_hbm)
+
+    def entry(w, k):
+        return halves[k] if w == 3 and k in halves else table[k]
 
     def start(w, *numbers):
         for k in numbers:
-            owner, which, target, _ = table[k]
-            src = ins[w] if k < 4 else rows(w, owner, which)
-            go(src, rows(w, owner, which), gs.at[w, k], gr.at[w, k], "dp", target)
+            mine, which, target, theirs = entry(w, k)
+            src = rows(w, mine, which)
+            if mine == (0, 0, 0):
+                src = ins[w].at[pl.ds({"w": 0, "a": 0, "b": cut}[which], {"w": depth, "a": cut, "b": depth - cut}[which])]
+            dst = rows(w, theirs if w == 3 else mine, which)
+            go(src, dst, gs.at[w, k], gr.at[w, k], "dp", target)
 
     def wait(w, *numbers):
         for k in numbers:
-            _, which, _, owner = table[k]
-            got(rows(w, owner, which), gs.at[w, k], gr.at[w, k])
-
-    own_copies = [pltpu.make_async_copy(ins[w], rows(w, me, "w"), ls.at[4 + w]) for w in range(4)]
-
-    def stage_a(w):
-        wait(w, 3)
-        start(w, 4, 5, 6)
-        wait(w, 1)
-        start(w, 7, 9)
-        wait(w, 2)
-        start(w, 8, 10)
-
-    def stage_b(w):
-        wait(w, 7)
-        start(w, 13)
-        wait(w, 8)
-        start(w, 14, 15)
-        wait(w, 4)
-        start(w, 11)
-        wait(w, 5)
-        start(w, 12)
-
-    def stage_c(w):
-        wait(w, 13, 14)
-        start(w, 16)
+            _, which, _, came = entry(w, k)
+            got(rows(w, came, which), gs.at[w, k], gr.at[w, k])
+
+    own_copies = [pltpu.make_async_copy(ins[w], rows(w, (0, 0, 0), "w"), ls.at[4 + w]) for w in range(4)]
 
     late = {0: (0, 6), -1: (9, 11), 1: (10, 12), 2: (15, 16)}
 
@@ -195,9 +190,9 @@
 
     start(0, 1, 2, 3, 0)
     own_copies[0].start()
-    go(seg_hbm, seg_prev, ms.at[0], mr.at[0], "dp", after)
     start(1, 1, 2, 3, 0)
     own_copies[1].start()
+    go(seg_hbm, seg_prev, ms.at[0], mr.at[0], "dp", after)
 
     loads[0].wait()
     for r in range(4):
@@ -216,33 +211,68 @@
     loads[1].wait()
     turn(tgt, tgt_t)
 
-    stage_a(0)
+    def near(w):
+        wait(w, 1)
+        start(w, 7, 9)
+        wait(w, 2)
+        start(w, 8, 10)
+        wait(w, 3)
+        start(w, 6)
+
+    def far(w):
+        wait(w, 7)
+        start(w, 13)
+        wait(w, 8)
+        start(w, 14, 15)
+
+    def diagonal(w):
+        wait(w, 4)
+        start(w, 11)
+        wait(w, 5)
+        start(w, 12)
+
+    def last(w):
+        wait(w, 13, 14)
+        start(w, 16)
+
+    near(0)
+    start(0, 4, 5)
     start(2, 1, 2, 3, 0)
     own_copies[2].start()
-    stage_a(1)
-    stage_b(0)
+    start(3, 3, 0)
+    own_copies[3].start()
+    near(1)
+    far(0)
+    diagonal(0)
     use(0, 0)
-    stage_a(2)
-    start(3, 1, 2)
-    own_copies[3].start()
-    stage_b(1)
+    near(2)
+    start(1, 4, 5)
+    start(2, 4, 5)
+    start(3, 1, 2, 17, 18)
+    far(1)
     use(1, 0)
-    stage_c(0)
+    last(0)
     use(0, -1)
     use(0, 1)
-    stage_b(2)
-    start(3, 3, 0)
+    far(2)
+    use(0, 2)
     use(2, 0)
-    stage_c(1)
+    diagonal(1)
+    wait(3, 3)
+    start(3, 6)
+    last(1)
     use(1, -1)
     use(1, 1)
-    use(0, 2)
+    use(1, 2)
+    diagonal(2)
+    last(2)
     use(2, -1)
     use(2, 1)
-    use(1, 2)
-    stage_c(2)
-    stage_a(3)
     use(2, 2)
+    wait(3, 1)
+    start(3, 7)
+    wait(3, 2)
+    start(3, 8)
 
     loads[2].wait()
     got(seg_prev, ms.at[0], mr.at[0])
@@ -270,24 +300,23 @@
 
     lax.fori_loop(0, tok_rows // 16, pointwise, 0)
 
-    order = (0, -1, 1, 2)
-
-    def out_piece(rel):
-        wait(3, *late[rel])
-        if rel == 0:
+    def out_piece(q):
+        if q == 0:
             own_copies[3].wait()
+            wait(3, 0, 6)
+        else:
+            wait(3, *{1: (9, 10), 2: (11, 12), 3: (15, 16)}[q])
 
         def chunk(n, _):
-            r = pl.ds(pl.multiple_of(piece_of(rel) * piece + n * depth, 16), depth)
+            r = pl.ds(pl.multiple_of(q * piece + n * 2 * depth, 16), 2 * depth)
             p[r] = dot_nt(full[3, r], stacked[...]).astype(bf)
             return 0
 
-        lax.fori_loop(0, 4, chunk, 0)
+        lax.fori_loop(0, 2, chunk, 0)
 
     def x_src(q):
         def src(chunk, lo, size):
-            r = pl.ds(pl.multiple_of(piece_of(order[q]) * piece + lo, 16), size)
-            return p.at[r, pl.ds(pl.multiple_of(((x + chunk) % 4) * 128, 128), 128)]
+            return p.at[pl.ds(q * piece + lo, size), pl.ds(pl.multiple_of(((x + chunk) % 4) * 128, 128), 128)]
 
         return src
 
@@ -296,6 +325,14 @@
             return xc.at[q, pl.ds(pl.multiple_of(((zh + chunk) % 4) * depth + lo, 16), size)]
 
         return src
+
+    def block_owner(q, j):
+        hi, lo = j // 2, j % 2
+        if q == 0:
+            return at(0, hi, lo)
+        if q == 3:
+            return at(2, hi, lo)
+        return at(2 * hi - 1, q - 1, lo)
 
     def ring1(q, src, size, mid, inbox, s, r, plus1, minus1):
         rest = size - mid
@@ -320,7 +357,7 @@
         return plus(src(0, 0, size)[...], inbox[q, 1], inbox[q, 2])
 
     def g_block(q, lo, size, chunk):
-        r = pl.ds(pl.multiple_of(piece_of(order[q]) * piece + lo, 16), size)
+        r = pl.ds(pl.multiple_of(q * piece + lo, 16), size)
         return gt.at[r, pl.ds(pl.multiple_of(((x + chunk) % 4) * 128, 128), 128)]
 
     def send_g(q, i, ref, target):
@@ -328,6 +365,9 @@
 
     def got_g(q, i, ref):
         got(ref, s4.at[q, i], r4.at[q, i])
+
+    def z_peer(k):
+        return (zh + k) % 4
 
     def step(i, q):
         half = piece // 2
@@ -337,72 +377,90 @@
             ring2(q, x_src(q), piece, half, xin, xtx, sx, rx, right, left)
         if i == 2:
             xc[q] = ring3(q, x_src(q), piece, half, xin, sx, rx).astype(bf)
-            ring1(q, z_src(q), depth, cut, zin, sz, rz, above, below)
+            for k in (2, 1, 3):
+                go(z_src(q)(k, 0, depth), zin.at[q, k - 1], sz.at[q, k], rz.at[q, k], "shard", z_peer(k) * 4 + x)
         if i == 3:
-            ring2(q, z_src(q), depth, cut, zin, ztx, sz, rz, above, below)
-        if i == 4:
-            total = ring3(q, z_src(q), depth, cut, zin, sz, rz)
+            for k in (1, 3, 2):
+                got(zin.at[q, k - 1], sz.at[q, k], rz.at[q, k])
+            total = plus(z_src(q)(0, 0, depth)[...], zin[q, 0], zin[q, 1], zin[q, 2])
             lanes = pl.ds(pl.multiple_of((x % 2) * 128, 128), 128)
-            r = pl.ds(pl.multiple_of(piece_of(order[q]) * piece + zh * depth, 16), depth)
+            r = pl.ds(pl.multiple_of(block_owner(q, zh) * depth, 16), depth)
             is_out = (1 - x // 2).astype(jnp.float32)
             wanted = tgt_t[r, lanes].astype(jnp.float32) * is_out
             mine = g_block(q, zh * depth, depth, 0)
             mine[...] = (keep[0:1, lanes] * (total - wanted)).astype(bf)
-            send_g(q, 0, mine, above)
-            send_g(q, 1, mine, below)
-        if i == 5:
-            lo, hi = ((zh + 3) % 4) * depth, ((zh + 1) % 4) * depth
-            got_g(q, 0, g_block(q, lo, depth, 0))
-            send_g(q, 2, g_block(q, lo, cut, 0), above)
-            got_g(q, 1, g_block(q, hi, depth, 0))
-            send_g(q, 3, g_block(q, hi + cut, depth - cut, 0), below)
-        if i == 6:
-            far = ((zh + 2) % 4) * depth
-            got_g(q, 2, g_block(q, far, cut, 0))
-            got_g(q, 3, g_block(q, far + cut, depth - cut, 0))
+            for k in (2, 1, 3):
+                send_g(q, k, mine, z_peer(k) * 4 + x)
+        if i == 4:
+            for k in (1, 3, 2):
+                got_g(q, k, g_block(q, z_peer(4 - k) * depth, depth, 0))
             send_g(q, 4, g_block(q, 0, piece, 0), right)
             send_g(q, 5, g_block(q, 0, piece, 0), left)
-        if i == 7:
+        if i == 5:
             got_g(q, 4, g_block(q, 0, piece, 3))
             send_g(q, 6, g_block(q, 0, half, 3), right)
             got_g(q, 5, g_block(q, 0, piece, 1))
             send_g(q, 7, g_block(q, half, half, 1), left)
-        if i == 8:
+        if i == 6:
             got_g(q, 6, g_block(q, 0, half, 2))
             got_g(q, 7, g_block(q, half, half, 2))
 
-            def chunk(n, _):
-                c = pl.ds(pl.multiple_of(n * 384, 128), 384)
-                term = dot_tn(gt[piece_rows(order[q])], full[3, piece_rows(order[q]), c])
-                if q == 0:
-                    back[:, c] = term
-                else:
-                    back[:, c] += term
-                return 0
-
-            lax.fori_loop(0, cols // 384, chunk, 0)
+    def back_piece(q):
+        def chunk(n, _):
+            c = pl.ds(pl.multiple_of(n * 384, 128), 384)
+            term = dot_tn(gt[q * piece : (q + 1) * piece], full[3, q * piece : (q + 1) * piece, c])
+            if q == 0:
+                back[:, c] = term
+            else:
+                back[:, c] += term
+            return 0
+
+        lax.fori_loop(0, cols // 384, chunk, 0)
 
     out_piece(0)
     step(0, 0)
-    stage_b(3)
-    out_piece(-1)
+    wait(3, 17)
+    start(3, 9)
+    wait(3, 18)
+    start(3, 10)
+    start(3, 4, 5)
+    out_piece(1)
+    step(1, 0)
     step(0, 1)
-    step(1, 0)
-    out_piece(1)
+    far(3)
+    step(2, 0)
+    step(1, 1)
+    diagonal(3)
+    out_piece(2)
     step(0, 2)
-    step(1, 1)
-    step(2, 0)
-    stage_c(3)
+    last(3)
+    step(2, 1)
+    out_piece(3)
+    step(0, 3)
     step(3, 0)
-    step(2, 1)
     step(1, 2)
-    out_piece(2)
-    step(0, 3)
-    for t in range(4, 12):
-        for q in range(4):
-            i = t - q
-            if 0 <= i < 9:
-                step(i, q)
+    step(3, 1)
+    step(1, 3)
+    step(2, 2)
+    step(4, 0)
+    step(4, 1)
+    step(2, 3)
+    step(3, 2)
+    step(5, 0)
+    step(3, 3)
+    step(5, 1)
+    step(6, 0)
+    back_piece(0)
+    step(4, 2)
+    step(6, 1)
+    back_piece(1)
+    step(4, 3)
+    step(5, 2)
+    step(5, 3)
+    step(6, 2)
+    back_piece(2)
+    step(6, 3)
+    back_piece(3)
 
     loads[3].wait()
     got(tok_t2, ms.at[1], mr.at[1])
@@ -481,10 +539,14 @@
 
         lax.fori_loop(0, tok_rows // 32, combine, 0)
         go(tgg.at[:, pc(q)], tgg2.at[:, pc(q)], ms.at[2 + q], mr.at[2 + q], "dp", sib)
-    for t in range(4 + PARTS - 1):
-        for q in range(PARTS):
-            if 0 <= t - q < 4:
-                reduce_step(t - q, q)
+    for q in range(PARTS):
+        reduce_step(0, q)
+    for q in range(PARTS):
+        reduce_step(1, q)
+    for q in range(PARTS):
+        reduce_step(2, q)
+    for q in range(PARTS):
+        reduce_step(3, q)
     for copy in sent:
         copy.wait_send()
 
@@ -496,7 +558,7 @@
     piece = 4 * depth
     cut = (depth // 32 + 1) * 16
     vm, dma = pltpu.VMEM, pltpu.SemaphoreType.DMA
-    anywhere = pl.BlockSpec(memory_space=pl.ANY)
+    anywhere = pl.BlockSpec(memory_space=pltpu.HBM)
     scratch = [
         vm((4, width, cols), bf),
         vm((tok_rows, width), bf),
@@ -517,7 +579,6 @@
         vm((4, piece, 128), bf),
         vm((4, piece, 128), bf),
         vm((4, 3, depth, 128), bf),
-        vm((4, depth, 128), bf),
         vm((tok_rows, cols), bf),
         vm((tok_rows, cols), bf),
         vm((8 * depth, cols), bf),
@@ -545,7 +606,7 @@
         out_specs=pl.BlockSpec(memory_space=pltpu.VMEM),
         scratch_shapes=scratch,
         compiler_params=pltpu.CompilerParams(
-            collective_id=1, has_side_effects=True, vmem_limit_bytes=62 * 2**20
+            collective_id=1, has_side_effects=True, vmem_limit_bytes=56 * 2**20
         ),
     )(tokens, target, segments[None], gate_weight, up_weight, vector, down_weight, gradient)
 

time: 182 us -> 156 us (0.86)
  Pallas kernels: 178 us -> 153 us
    pallas_call x1, Pallas kernels: 178 us -> 153 us  [per_device(): pl.pallas_call(functools.partial(step_kernel, (tok_rows, width, depth, co...]
where the time goes in v3:
time: 156 us; the launch traced here: 155 us
  Pallas kernels  153 us (98%)
  local copies, waits for them, and re-layouts  1.73 us (1%)
    pallas_call x1, Pallas kernels, per_device(): pl.pallas_call(functools.partial(step_kernel, (tok_rows, width, depth, co...  153 us

profile of v3, /device:TPU:1, one launch (start us, length us, event | category | flops | bytes accessed | tf_op | source)
XLA Modules:
  0.0 155.2 jit_solution(10202638504270261928)
XLA Ops:
  0.0 153.4 %shard_map.82 = bf16[144,1152]{1,0:T(8,128)(2,1)} custom-call(bf16[256,2304]{1,0:T(8,128)(2,1)} %tok_hbm.1, bf16[256,2304]{1,0:T(8,128)(2,1)} %tgt_hbm.1, s32[1,256]{1,0:T(1,128)} %bitcast.1, bf16[144,1152]{1,0:T(8,128)(2,1)} %gate_hbm.1, bf16[144,1152]{1,0:T(8,128)(2,1)} %up_hbm.1, bf16[144,1152]{1,0:T(8,128)(2,1)} %vec_hbm.1, bf16[144,1152]{1,0:T(8,128)(2,1)} %down_hbm.1, ...), custom_call_target="tpu_custom_call" | custom-call | tf_op jit(solution)/shard_map/pallas_call | solution.py:602
  153.5 1.7 %copy.10 = bf16[144,1152]{1,0:T(8,128)(2,1)} copy(bf16[144,1152]{1,0:T(8,128)(2,1)} %shard_map.82) | data formatting | bytes 663552

commit v4 on v3

--- a/solution.py
+++ b/solution.py
@@ -64,9 +64,9 @@
 
 def step_kernel(
     dims, tok_hbm, tgt_hbm, seg_hbm, gate_hbm, up_hbm, vec_hbm, down_hbm, grad_hbm, o_ref,
-    full, tok, tgt, tok4, tok_t, tok_t2, tgt_t, seg, seg_prev, keep, acc, stacked, p, back, gt,
-    xin, xtx, xc, zin, tgg, tgg2, cp, cin, cout, grad,
-    gs, gr, sx, rx, sz, rz, s4, r4, cs, cr, ms, mr, ls,
+    half, full, tok, tgt, tok4, tokp, tok_t, tok_t2, tgt_t, seg, seg_prev, keep, acc, accp, resb, resr, fac, stacked, p, back, gt,
+    xin, xtx, xc, zin, tgg, tgg2, cp, cin, cout, grad, vec,
+    gs, gr, sx, rx, sz, rz, s4, r4, cs, cr, ms, mr, ts, tr, ls,
 ):
     tok_rows, width, depth, cols = dims
     bf = jnp.bfloat16
@@ -75,6 +75,8 @@
     x, zh = sh % 4, sh // 4
     piece = 4 * depth
     cut = (depth // 32 + 1) * 16
+    wide = -(-cols // 256) * 128
+    rem = cols - wide
     part = cols // PARTS
     inv_root = float(width) ** (-0.5)
 
@@ -93,7 +95,7 @@
 
     loads = [
         pltpu.make_async_copy(src, dst, ls.at[i])
-        for i, (src, dst) in enumerate(((tok_hbm, tok), (tgt_hbm, tgt), (seg_hbm, seg), (grad_hbm, grad)))
+        for i, (src, dst) in enumerate(((tok_hbm, tok), (tgt_hbm, tgt), (seg_hbm, seg), (grad_hbm, grad), (vec_hbm, vec)))
     ]
     for copy in loads:
         copy.start()
@@ -112,10 +114,19 @@
     def place(dy, dz, dc):
         return {0: 2 * dz, -1: 4 + 4 * dz, 1: 6 + 4 * dz, 2: 12 + 2 * dz}[dy] + dc
 
+    extent = {"w": (0, depth), "a": (0, cut), "b": (cut, depth - cut)}
+
     def rows(w, rel, which):
-        lo, size = {"w": (0, depth), "a": (0, cut), "b": (cut, depth - cut)}[which]
+        lo, size = extent[which]
         base = place(*rel) if w == 3 else at(*rel)
-        return full.at[w, pl.ds(pl.multiple_of(base * depth + lo, 16), size)]
+        r = pl.ds(pl.multiple_of(base * depth + lo, 16), size)
+        return full.at[r] if w == 3 else half.at[w, r]
+
+    def own_part(w, which, z_of):
+        lo, size = extent[which]
+        if w == 3:
+            return ins[w].at[pl.ds(lo, size)]
+        return ins[w].at[pl.ds(lo, size), pl.ds(pl.multiple_of(z_of * rem, 128), wide)]
 
     me = at(0, 0, 0)
     table = [
@@ -137,7 +148,7 @@
         ((2, 0, 0), "w", sib, (2, 0, 1)),
         ((2, 1, 0), "w", sib, (2, 1, 1)),
     ]
-    halves = {
+    special_down = {
         1: ((0, 0, 0), "a", up, (-1, 0, 0)),
         2: ((0, 0, 0), "b", down, (1, 0, 0)),
         17: ((0, 0, 0), "b", up, (-1, 0, 0)),
@@ -145,15 +156,21 @@
     }
     ins = (gate_hbm, up_hbm, vec_hbm, down_hbm)
 
+    special_half = {
+        13: ((-1, 1, 0), "a", up, (2, 1, 0)),
+        14: ((1, 1, 0), "b", down, (2, 1, 0)),
+    }
+
     def entry(w, k):
-        return halves[k] if w == 3 and k in halves else table[k]
+        special = special_down if w == 3 else special_half
+        return special[k] if k in special else table[k]
 
     def start(w, *numbers):
         for k in numbers:
             mine, which, target, theirs = entry(w, k)
             src = rows(w, mine, which)
             if mine == (0, 0, 0):
-                src = ins[w].at[pl.ds({"w": 0, "a": 0, "b": cut}[which], {"w": depth, "a": cut, "b": depth - cut}[which])]
+                src = own_part(w, which, (zl + (k == 3)) % 2)
             dst = rows(w, theirs if w == 3 else mine, which)
             go(src, dst, gs.at[w, k], gr.at[w, k], "dp", target)
 
@@ -162,7 +179,7 @@
             _, which, _, came = entry(w, k)
             got(rows(w, came, which), gs.at[w, k], gr.at[w, k])
 
-    own_copies = [pltpu.make_async_copy(ins[w], rows(w, (0, 0, 0), "w"), ls.at[4 + w]) for w in range(4)]
+    own_copies = [pltpu.make_async_copy(own_part(w, "w", zl), rows(w, (0, 0, 0), "w"), ls.at[5 + w]) for w in range(4)]
 
     late = {0: (0, 6), -1: (9, 11), 1: (10, 12), 2: (15, 16)}
 
@@ -172,21 +189,43 @@
     def piece_rows(rel):
         return pl.ds(pl.multiple_of(piece_of(rel) * piece, 16), piece)
 
-    def use(w, rel):
+    came_in = set()
+
+    def settle(w, rel):
+        if (w, rel) in came_in:
+            return
+        came_in.add((w, rel))
         wait(w, *late[rel])
         if rel == 0:
             own_copies[w].wait()
 
-        def chunk(n, _):
-            c = pl.ds(pl.multiple_of(n * 384, 128), 384)
-            term = dot_nn(tok4[piece_of(rel)], full[w, piece_rows(rel), c])
+    def use(w, rel):
+        settle(w, rel)
+        for c in (slice(0, 384), slice(384, wide)):
+            term = dot_nn(tok4[piece_of(rel)], half[w, piece_rows(rel), c])
             if rel == 0:
                 acc[w, :, c] = term
             else:
                 acc[w, :, c] += term
+
+    def use_for_partner(w, rel):
+        settle(w, rel)
+
+        def chunk(n, _):
+            c = pl.ds(pl.multiple_of(n * (rem // 2), 128), rem // 2)
+            c2 = pl.ds(pl.multiple_of(zl * (wide - rem) + n * (rem // 2), 128), rem // 2)
+            term = dot_nn(tokp[piece_of(rel)], half[w, piece_rows(rel), c2])
+            if rel == 0:
+                accp[w, :, c] = term
+            else:
+                accp[w, :, c] += term
+            if rel == 2:
+                resb[w, :, c] = accp[w, :, c].astype(bf)
             return 0
 
-        lax.fori_loop(0, cols // 384, chunk, 0)
+        lax.fori_loop(0, 2, chunk, 0)
+        if rel == 2:
+            go(resb.at[w], resr.at[w], ts.at[5 + w], tr.at[5 + w], "dp", zed)
 
     start(0, 1, 2, 3, 0)
     own_copies[0].start()
@@ -197,6 +236,11 @@
     loads[0].wait()
     for r in range(4):
         tok4[r] = tok[:, r * piece : (r + 1) * piece]
+    go(tok4.at[x], tokp.at[x], ts.at[0], tr.at[0], "dp", zed)
+    start(2, 3, 0)
+    own_copies[2].start()
+    start(3, 3, 0)
+    own_copies[3].start()
 
     def turn(src, dst):
         def body(j, _):
@@ -208,22 +252,35 @@
 
     turn(tok, tok_t)
     go(tok_t, tok_t2, ms.at[1], mr.at[1], "dp", sib)
-    loads[1].wait()
-    turn(tgt, tgt_t)
+
+    def tokens_start():
+        got(tokp.at[x], ts.at[0], tr.at[0])
+        go(tokp.at[x], tokp.at[x], ts.at[1], tr.at[1], "shard", right)
+        go(tokp.at[x], tokp.at[x], ts.at[2], tr.at[2], "shard", left)
+
+    def tokens_relay():
+        h = tok_rows // 2
+        got(tokp.at[(x + 3) % 4], ts.at[1], tr.at[1])
+        ref = tokp.at[(x + 3) % 4, pl.ds(0, h)]
+        go(ref, ref, ts.at[3], tr.at[3], "shard", right)
+        got(tokp.at[(x + 1) % 4], ts.at[2], tr.at[2])
+        ref = tokp.at[(x + 1) % 4, pl.ds(h, h)]
+        go(ref, ref, ts.at[4], tr.at[4], "shard", left)
+
+    def tokens_end():
+        h = tok_rows // 2
+        got(tokp.at[(x + 2) % 4, pl.ds(0, h)], ts.at[3], tr.at[3])
+        got(tokp.at[(x + 2) % 4, pl.ds(h, h)], ts.at[4], tr.at[4])
+
+    def near_z(w):
+        wait(w, 3)
+        start(w, 4, 5, 6)
 
     def near(w):
         wait(w, 1)
         start(w, 7, 9)
         wait(w, 2)
         start(w, 8, 10)
-        wait(w, 3)
-        start(w, 6)
-
-    def far(w):
-        wait(w, 7)
-        start(w, 13)
-        wait(w, 8)
-        start(w, 14, 15)
 
     def diagonal(w):
         wait(w, 4)
@@ -231,48 +288,68 @@
         wait(w, 5)
         start(w, 12)
 
+    def round_z(w):
+        wait(w, 4)
+        start(w, 13, 11)
+        wait(w, 5)
+        start(w, 14, 12)
+
+    def far(w):
+        wait(w, 7, 8)
+        start(w, 15)
+
     def last(w):
         wait(w, 13, 14)
         start(w, 16)
 
+    near_z(0)
     near(0)
-    start(0, 4, 5)
-    start(2, 1, 2, 3, 0)
-    own_copies[2].start()
-    start(3, 3, 0)
-    own_copies[3].start()
+    start(2, 1, 2)
+    loads[1].wait()
+    turn(tgt, tgt_t)
+    round_z(0)
+    near_z(1)
     near(1)
+    tokens_start()
+    near_z(2)
+    use(0, 0)
     far(0)
-    diagonal(0)
-    use(0, 0)
+    use(0, -1)
+    use(0, 1)
+    last(0)
+    round_z(1)
     near(2)
-    start(1, 4, 5)
-    start(2, 4, 5)
+    tokens_relay()
+    use(0, 2)
+    use(1, 0)
+    round_z(2)
     start(3, 1, 2, 17, 18)
     far(1)
-    use(1, 0)
-    last(0)
-    use(0, -1)
-    use(0, 1)
+    tokens_end()
+    use_for_partner(0, 0)
+    use_for_partner(0, -1)
+    use_for_partner(0, 1)
+    use_for_partner(0, 2)
+    last(1)
     far(2)
-    use(0, 2)
-    use(2, 0)
-    diagonal(1)
-    wait(3, 3)
-    start(3, 6)
-    last(1)
+    use_for_partner(1, 0)
+    use_for_partner(1, -1)
+    use_for_partner(1, 1)
+    use_for_partner(1, 2)
+    last(2)
+    use_for_partner(2, 0)
+    use_for_partner(2, -1)
+    use_for_partner(2, 1)
+    use_for_partner(2, 2)
     use(1, -1)
     use(1, 1)
     use(1, 2)
-    diagonal(2)
-    last(2)
+    use(2, 0)
     use(2, -1)
     use(2, 1)
     use(2, 2)
-    wait(3, 1)
-    start(3, 7)
-    wait(3, 2)
-    start(3, 8)
+    wait(3, 3)
+    start(3, 6)
 
     loads[2].wait()
     got(seg_prev, ms.at[0], mr.at[0])
@@ -286,19 +363,39 @@
     first = (lane + d) == 0
     keep[...] = jnp.where(first, 0.0, jnp.where(here == previous, 1.0, 0.0))
 
-    def pointwise(i, _):
-        r = pl.ds(pl.multiple_of(i * 16, 16), 16)
-        r2 = pl.ds(pl.multiple_of(tok_rows + i * 16, 16), 16)
-        value, slope, curve = gelu_parts(acc[0, r])
-        up_act = acc[1, r]
-        tangent = acc[2, r] * inv_root
-        stacked[r] = (value * up_act).astype(bf)
-        stacked[r2] = (slope * tangent * up_act).astype(bf)
-        acc[0, r] = up_act * slope
-        acc[1, r] = up_act * curve * tangent
-        return 0
-
-    lax.fori_loop(0, tok_rows // 16, pointwise, 0)
+    def pointwise(c, parts_of):
+        def body(i, _):
+            r = pl.ds(pl.multiple_of(i * 16, 16), 16)
+            r2 = pl.ds(pl.multiple_of(tok_rows + i * 16, 16), 16)
+            pre_gate, up_act, tangent_raw = parts_of(r)
+            value, slope, curve = gelu_parts(pre_gate)
+            tangent = tangent_raw * inv_root
+            stacked[r, c] = (value * up_act).astype(bf)
+            stacked[r2, c] = (slope * tangent * up_act).astype(bf)
+            fac[0, r, c] = up_act * slope
+            fac[1, r, c] = up_act * curve * tangent
+            return 0
+
+        lax.fori_loop(0, tok_rows // 16, body, 0)
+
+    pointwise(
+        pl.ds(pl.multiple_of(zl * rem, 128), wide), lambda r: [acc[w, r] for w in range(3)]
+    )
+    wait(3, 1)
+    start(3, 7)
+    wait(3, 2)
+    start(3, 8)
+    start(3, 4, 5)
+    wait(3, 17)
+    start(3, 9)
+    wait(3, 18)
+    start(3, 10)
+    for w in range(3):
+        got(resr.at[w], ts.at[5 + w], tr.at[5 + w])
+    pointwise(
+        pl.ds(pl.multiple_of((1 - zl) * wide, 128), rem),
+        lambda r: [resr[w, r].astype(jnp.float32) for w in range(3)],
+    )
 
     def out_piece(q):
         if q == 0:
@@ -309,7 +406,7 @@
 
         def chunk(n, _):
             r = pl.ds(pl.multiple_of(q * piece + n * 2 * depth, 16), 2 * depth)
-            p[r] = dot_nt(full[3, r], stacked[...]).astype(bf)
+            p[r] = dot_nt(full[r], stacked[...]).astype(bf)
             return 0
 
         lax.fori_loop(0, 2, chunk, 0)
@@ -408,7 +505,7 @@
     def back_piece(q):
         def chunk(n, _):
             c = pl.ds(pl.multiple_of(n * 384, 128), 384)
-            term = dot_tn(gt[q * piece : (q + 1) * piece], full[3, q * piece : (q + 1) * piece, c])
+            term = dot_tn(gt[q * piece : (q + 1) * piece], full[q * piece : (q + 1) * piece, c])
             if q == 0:
                 back[:, c] = term
             else:
@@ -419,25 +516,23 @@
 
     out_piece(0)
     step(0, 0)
-    wait(3, 17)
-    start(3, 9)
-    wait(3, 18)
-    start(3, 10)
-    start(3, 4, 5)
     out_piece(1)
+    step(0, 1)
+    wait(3, 7)
+    start(3, 13)
+    wait(3, 8)
+    start(3, 14, 15)
     step(1, 0)
-    step(0, 1)
-    far(3)
     step(2, 0)
+    diagonal(3)
     step(1, 1)
-    diagonal(3)
     out_piece(2)
     step(0, 2)
+    step(2, 1)
     last(3)
-    step(2, 1)
+    step(3, 0)
     out_piece(3)
     step(0, 3)
-    step(3, 0)
     step(1, 2)
     step(3, 1)
     step(1, 3)
@@ -450,11 +545,11 @@
     step(3, 3)
     step(5, 1)
     step(6, 0)
+    step(4, 2)
     back_piece(0)
-    step(4, 2)
     step(6, 1)
+    step(4, 3)
     back_piece(1)
-    step(4, 3)
     step(5, 2)
     step(5, 3)
     step(6, 2)
@@ -463,6 +558,7 @@
     back_piece(3)
 
     loads[3].wait()
+    loads[4].wait()
     got(tok_t2, ms.at[1], mr.at[1])
 
     def pc(q):
@@ -522,7 +618,7 @@
             got_c(box(5, q), 6, q)
             got_c(box(6, q), 7, q)
             total = plus(c_block(0, 0, q)[...], box(4, q)[...], box(5, q)[...], box(6, q)[...])
-            own = full[2, pl.ds(pl.multiple_of(me * depth, 16), depth), pc(q)]
+            own = vec[:, pc(q)]
             o_ref[:, pc(q)] = (
                 grad[:, pc(q)].astype(jnp.float32)
                 + (1.0 - damping) * own.astype(jnp.float32)
@@ -534,7 +630,7 @@
         def combine(i, _):
             r = pl.ds(pl.multiple_of(i * 32, 16), 32)
             r2 = pl.ds(pl.multiple_of(tok_rows + i * 32, 16), 32)
-            tgg[r, pc(q)] = (acc[0, r, pc(q)] * back[r2, pc(q)] + acc[1, r, pc(q)] * back[r, pc(q)]).astype(bf)
+            tgg[r, pc(q)] = (fac[0, r, pc(q)] * back[r2, pc(q)] + fac[1, r, pc(q)] * back[r, pc(q)]).astype(bf)
             return 0
 
         lax.fori_loop(0, tok_rows // 32, combine, 0)
@@ -557,12 +653,15 @@
     bf, f32 = jnp.bfloat16, jnp.float32
     piece = 4 * depth
     cut = (depth // 32 + 1) * 16
+    wide = -(-cols // 256) * 128
     vm, dma = pltpu.VMEM, pltpu.SemaphoreType.DMA
     anywhere = pl.BlockSpec(memory_space=pltpu.HBM)
     scratch = [
-        vm((4, width, cols), bf),
+        vm((3, width, wide), bf),
+        vm((width, cols), bf),
         vm((tok_rows, width), bf),
         vm((tok_rows, width), bf),
+        vm((4, tok_rows, piece), bf),
         vm((4, tok_rows, piece), bf),
         vm((width, tok_rows), bf),
         vm((width, tok_rows), bf),
@@ -570,7 +669,11 @@
         vm((1, tok_rows), jnp.int32),
         vm((1, tok_rows), jnp.int32),
         vm((8, tok_rows), f32),
-        vm((3, tok_rows, cols), f32),
+        vm((3, tok_rows, wide), f32),
+        vm((3, tok_rows, cols - wide), f32),
+        vm((3, tok_rows, cols - wide), bf),
+        vm((3, tok_rows, cols - wide), bf),
+        vm((2, tok_rows, cols), f32),
         vm((2 * tok_rows, cols), bf),
         vm((width, 2 * tok_rows), bf),
         vm((2 * tok_rows, cols), f32),
@@ -585,6 +688,7 @@
         vm((7, depth, cols), bf),
         vm((4, depth, cols), bf),
         vm((depth, cols), bf),
+        vm((depth, cols), bf),
         dma((4, GATHER_COPIES)),
         dma((4, GATHER_COPIES)),
         dma((4, 6)),
@@ -598,6 +702,8 @@
         dma((2 + PARTS,)),
         dma((2 + PARTS,)),
         dma((8,)),
+        dma((8,)),
+        dma((9,)),
     ]
     return pl.pallas_call(
         functools.partial(step_kernel, (tok_rows, width, depth, cols)),

time: 156 us -> 145 us (0.929)
  Pallas kernels: 153 us -> 143 us
    pallas_call x1, Pallas kernels: 153 us -> 143 us  [per_device(): pl.pallas_call(functools.partial(step_kernel, (tok_rows, width, depth, co...]
where the time goes in v4:
time: 145 us; the launch traced here: 144 us
  Pallas kernels  143 us (99%)
  local copies, waits for them, and re-layouts  1.73 us (1%)
    pallas_call x1, Pallas kernels, per_device(): pl.pallas_call(functools.partial(step_kernel, (tok_rows, width, depth, co...  143 us

profile of v4, /device:TPU:1, one launch (start us, length us, event | category | flops | bytes accessed | tf_op | source)
XLA Modules:
  0.0 144.4 jit_solution(12194812218142046220)
XLA Ops:
  0.0 142.6 %shard_map.82 = bf16[144,1152]{1,0:T(8,128)(2,1)} custom-call(bf16[256,2304]{1,0:T(8,128)(2,1)} %tok_hbm.1, bf16[256,2304]{1,0:T(8,128)(2,1)} %tgt_hbm.1, s32[1,256]{1,0:T(1,128)} %bitcast.1, bf16[144,1152]{1,0:T(8,128)(2,1)} %gate_hbm.1, bf16[144,1152]{1,0:T(8,128)(2,1)} %up_hbm.1, bf16[144,1152]{1,0:T(8,128)(2,1)} %vec_hbm.1, bf16[144,1152]{1,0:T(8,128)(2,1)} %down_hbm.1, ...), custom_call_target="tpu_custom_call" | custom-call | tf_op jit(solution)/shard_map/pallas_call | solution.py:708
  142.7 1.7 %copy.10 = bf16[144,1152]{1,0:T(8,128)(2,1)} copy(bf16[144,1152]{1,0:T(8,128)(2,1)} %shard_map.82) | data formatting | bytes 663552

commit v5 on v4

--- a/solution.py
+++ b/solution.py
@@ -41,6 +41,7 @@
 
 GATHER_COPIES = 19
 PARTS = 3
+PIECES = ((0, 4), (4, 4), (8, 4), (12, 4), (16, 4), (20, 4), (24, 4), (28, 4), (32, 4), (36, 4), (40, 4), (44, 4))
 
 
 def plus(a, *more):
@@ -66,7 +67,7 @@
     dims, tok_hbm, tgt_hbm, seg_hbm, gate_hbm, up_hbm, vec_hbm, down_hbm, grad_hbm, o_ref,
     half, full, tok, tgt, tok4, tokp, tok_t, tok_t2, tgt_t, seg, seg_prev, keep, acc, accp, resb, resr, fac, stacked, p, back, gt,
     xin, xtx, xc, zin, tgg, tgg2, cp, cin, cout, grad, vec,
-    gs, gr, sx, rx, sz, rz, s4, r4, cs, cr, ms, mr, ts, tr, ls,
+    gs, gr, sx, rx, cs, cr, ms, mr, ts, tr, ls,
 ):
     tok_rows, width, depth, cols = dims
     bf = jnp.bfloat16
@@ -103,10 +104,11 @@
 
     sent = []
 
-    def go(src, dst, s, r, axis, target):
+    def go(src, dst, s, r, axis, target, kept=True):
         copy = remote(src, dst, s, r, axis, target)
         copy.start()
-        sent.append(copy)
+        if kept:
+            sent.append(copy)
 
     def got(ref, s, r):
         remote(ref, ref, s, r, "dp", sib).wait_recv()
@@ -172,12 +174,12 @@
             if mine == (0, 0, 0):
                 src = own_part(w, which, (zl + (k == 3)) % 2)
             dst = rows(w, theirs if w == 3 else mine, which)
-            go(src, dst, gs.at[w, k], gr.at[w, k], "dp", target)
+            go(src, dst, gs.at[w], gr.at[w, k], "dp", target, False)
 
     def wait(w, *numbers):
         for k in numbers:
             _, which, _, came = entry(w, k)
-            got(rows(w, came, which), gs.at[w, k], gr.at[w, k])
+            got(rows(w, came, which), gs.at[w], gr.at[w, k])
 
     own_copies = [pltpu.make_async_copy(own_part(w, "w", zl), rows(w, (0, 0, 0), "w"), ls.at[5 + w]) for w in range(4)]
 
@@ -229,7 +231,7 @@
 
     start(0, 1, 2, 3, 0)
     own_copies[0].start()
-    start(1, 1, 2, 3, 0)
+    start(1, 1, 2, 0)
     own_copies[1].start()
     go(seg_hbm, seg_prev, ms.at[0], mr.at[0], "dp", after)
 
@@ -237,6 +239,7 @@
     for r in range(4):
         tok4[r] = tok[:, r * piece : (r + 1) * piece]
     go(tok4.at[x], tokp.at[x], ts.at[0], tr.at[0], "dp", zed)
+    start(1, 3)
     start(2, 3, 0)
     own_copies[2].start()
     start(3, 3, 0)
@@ -307,23 +310,22 @@
     start(2, 1, 2)
     loads[1].wait()
     turn(tgt, tgt_t)
+    tokens_start()
     round_z(0)
+    near(1)
     near_z(1)
-    near(1)
-    tokens_start()
-    near_z(2)
     use(0, 0)
     far(0)
     use(0, -1)
     use(0, 1)
+    tokens_relay()
+    round_z(1)
+    near_z(2)
     last(0)
-    round_z(1)
     near(2)
-    tokens_relay()
-    use(0, 2)
     use(1, 0)
-    round_z(2)
-    start(3, 1, 2, 17, 18)
+    use(2, 0)
+    use(1, -1)
     far(1)
     tokens_end()
     use_for_partner(0, 0)
@@ -331,25 +333,31 @@
     use_for_partner(0, 1)
     use_for_partner(0, 2)
     last(1)
-    far(2)
     use_for_partner(1, 0)
     use_for_partner(1, -1)
     use_for_partner(1, 1)
     use_for_partner(1, 2)
-    last(2)
     use_for_partner(2, 0)
+    round_z(2)
+    start(3, 1, 2, 17, 18)
+    use(0, 2)
+    use(1, 1)
+    use(1, 2)
+    far(2)
     use_for_partner(2, -1)
     use_for_partner(2, 1)
-    use_for_partner(2, 2)
-    use(1, -1)
-    use(1, 1)
-    use(1, 2)
-    use(2, 0)
+    last(2)
     use(2, -1)
     use(2, 1)
+    use_for_partner(2, 2)
     use(2, 2)
     wait(3, 3)
     start(3, 6)
+    wait(3, 1)
+    start(3, 7)
+    wait(3, 2)
+    start(3, 8)
+    start(3, 4, 5)
 
     loads[2].wait()
     got(seg_prev, ms.at[0], mr.at[0])
@@ -381,11 +389,6 @@
     pointwise(
         pl.ds(pl.multiple_of(zl * rem, 128), wide), lambda r: [acc[w, r] for w in range(3)]
     )
-    wait(3, 1)
-    start(3, 7)
-    wait(3, 2)
-    start(3, 8)
-    start(3, 4, 5)
     wait(3, 17)
     start(3, 9)
     wait(3, 18)
@@ -397,165 +400,240 @@
         lambda r: [resr[w, r].astype(jnp.float32) for w in range(3)],
     )
 
+    ready = set()
+
     def out_piece(q):
-        if q == 0:
-            own_copies[3].wait()
-            wait(3, 0, 6)
-        else:
-            wait(3, *{1: (9, 10), 2: (11, 12), 3: (15, 16)}[q])
+        row0, size = PIECES[q][0] * 48, PIECES[q][1] * 48
+        group = row0 // piece
+        if group not in ready:
+            ready.add(group)
+            if group == 0:
+                own_copies[3].wait()
+            wait(3, *{0: (0, 6), 1: (9, 10), 2: (11, 12), 3: (15, 16)}[group])
+        if size < piece:
+            r = pl.ds(row0, size)
+            p[r] = dot_nt(full[r], stacked[...]).astype(bf)
+            return
 
         def chunk(n, _):
-            r = pl.ds(pl.multiple_of(q * piece + n * 2 * depth, 16), 2 * depth)
+            r = pl.ds(pl.multiple_of(row0 + n * 2 * depth, 16), 2 * depth)
             p[r] = dot_nt(full[r], stacked[...]).astype(bf)
             return 0
 
         lax.fori_loop(0, 2, chunk, 0)
 
-    def x_src(q):
+    def x_src(row0):
         def src(chunk, lo, size):
-            return p.at[pl.ds(q * piece + lo, size), pl.ds(pl.multiple_of(((x + chunk) % 4) * 128, 128), 128)]
+            return p.at[pl.ds(row0 + lo, size), pl.ds(pl.multiple_of(((x + chunk) % 4) * 128, 128), 128)]
 
         return src
 
-    def z_src(q):
-        def src(chunk, lo, size):
-            return xc.at[q, pl.ds(pl.multiple_of(((zh + chunk) % 4) * depth + lo, 16), size)]
+    def z_src(row0, size):
+        def src(chunk):
+            return xc.at[pl.ds(pl.multiple_of(row0 + ((zh + chunk) % 4) * size, 16), size)]
 
         return src
 
-    def block_owner(q, j):
+    def block_owner(group, j):
         hi, lo = j // 2, j % 2
-        if q == 0:
+        if group == 0:
             return at(0, hi, lo)
-        if q == 3:
+        if group == 3:
             return at(2, hi, lo)
-        return at(2 * hi - 1, q - 1, lo)
-
-    def ring1(q, src, size, mid, inbox, s, r, plus1, minus1):
-        rest = size - mid
-        for i, (dst, frm, lo, n, target) in enumerate((
-            (0, 2, mid, rest, plus1), (0, 2, 0, mid, minus1), (1, 1, 0, mid, plus1), (2, 3, mid, rest, minus1),
-        )):
-            go(src(frm, lo, n), inbox.at[q, dst, pl.ds(lo, n)], s.at[q, i], r.at[q, i], "shard", target)
-
-    def ring2(q, src, size, mid, inbox, out, s, r, plus1, minus1):
-        rest = size - mid
-        for i, (dst, frm, lo, n, target) in enumerate(((1, 1, mid, rest, plus1), (2, 3, 0, mid, minus1))):
-            came = inbox.at[q, 0, pl.ds(lo, n)]
-            got(came, s.at[q, i], r.at[q, i])
-            out[q, lo : lo + n] = plus(src(frm, lo, n)[...], came[...]).astype(bf)
-            go(out.at[q, pl.ds(lo, n)], inbox.at[q, dst, pl.ds(lo, n)], s.at[q, 4 + i], r.at[q, 4 + i], "shard", target)
-
-    def ring3(q, src, size, mid, inbox, s, r):
-        got(inbox.at[q, 1, pl.ds(0, mid)], s.at[q, 2], r.at[q, 2])
-        got(inbox.at[q, 2, pl.ds(mid, size - mid)], s.at[q, 3], r.at[q, 3])
-        got(inbox.at[q, 1, pl.ds(mid, size - mid)], s.at[q, 4], r.at[q, 4])
-        got(inbox.at[q, 2, pl.ds(0, mid)], s.at[q, 5], r.at[q, 5])
-        return plus(src(0, 0, size)[...], inbox[q, 1], inbox[q, 2])
-
-    def g_block(q, lo, size, chunk):
-        r = pl.ds(pl.multiple_of(q * piece + lo, 16), size)
-        return gt.at[r, pl.ds(pl.multiple_of(((x + chunk) % 4) * 128, 128), 128)]
-
-    def send_g(q, i, ref, target):
-        go(ref, ref, s4.at[q, i], r4.at[q, i], "shard", target)
-
-    def got_g(q, i, ref):
-        got(ref, s4.at[q, i], r4.at[q, i])
+        return at(2 * hi - 1, group - 1, lo)
+
+    def g_block(lo, size, chunk):
+        return gt.at[pl.ds(pl.multiple_of(lo, 16), size), pl.ds(pl.multiple_of(((x + chunk) % 4) * 128, 128), 128)]
 
     def z_peer(k):
         return (zh + k) % 4
 
     def step(i, q):
-        half = piece // 2
+        row0, size = PIECES[q][0] * 48, PIECES[q][1] * 48
+        group, mid, sub = row0 // piece, size // 2, size // 4
+        src, zsrc = x_src(row0), z_src(row0, sub)
+        lower, upper = (0, mid), (mid, mid)
+
+        def inbox(dst, part):
+            return xin.at[dst, pl.ds(row0 + part[0], part[1])]
+
+        def send(k, frm, dst, target):
+            go(frm, dst, sx.at[0], rx.at[q, k], "shard", target, False)
+
+        def came(k, ref):
+            got(ref, sx.at[0], rx.at[q, k])
+
+        def zbox(k):
+            return zin.at[k - 1, pl.ds(row0 // 4, sub)]
+
+        two = xin.at[pl.ds(1, 2), pl.ds(row0, size)]
+        one = xin.at[0, pl.ds(row0, size)]
+        three = zin.at[:, pl.ds(row0 // 4, sub)]
+
         if i == 0:
-            ring1(q, x_src(q), piece, half, xin, sx, rx, right, left)
+            send(0, src(2, *upper), inbox(0, upper), right)
+            send(0, src(2, *lower), inbox(0, lower), left)
+            send(1, src(1, *lower), inbox(1, lower), right)
+            send(1, src(3, *upper), inbox(2, upper), left)
         if i == 1:
-            ring2(q, x_src(q), piece, half, xin, xtx, sx, rx, right, left)
+            came(0, one)
+            for part, frm, dst, target in ((upper, 1, 1, right), (lower, 3, 2, left)):
+                out = xtx.at[pl.ds(row0 + part[0], part[1])]
+                out[...] = plus(src(frm, *part)[...], inbox(0, part)[...]).astype(bf)
+                send(1, out, inbox(dst, part), target)
         if i == 2:
-            xc[q] = ring3(q, x_src(q), piece, half, xin, sx, rx).astype(bf)
+            came(1, two)
+            both = (0, size)
+            xc[row0 : row0 + size] = plus(src(0, *both)[...], inbox(1, both)[...], inbox(2, both)[...]).astype(bf)
             for k in (2, 1, 3):
-                go(z_src(q)(k, 0, depth), zin.at[q, k - 1], sz.at[q, k], rz.at[q, k], "shard", z_peer(k) * 4 + x)
+                send(2, zsrc(k), zbox(k), z_peer(k) * 4 + x)
         if i == 3:
-            for k in (1, 3, 2):
-                got(zin.at[q, k - 1], sz.at[q, k], rz.at[q, k])
-            total = plus(z_src(q)(0, 0, depth)[...], zin[q, 0], zin[q, 1], zin[q, 2])
+            came(2, three)
+            total = plus(zsrc(0)[...], zbox(1)[...], zbox(2)[...], zbox(3)[...])
             lanes = pl.ds(pl.multiple_of((x % 2) * 128, 128), 128)
-            r = pl.ds(pl.multiple_of(block_owner(q, zh) * depth, 16), depth)
+            row = row0 - group * piece + zh * sub
+            block = row // depth
+            r = pl.ds(pl.multiple_of(block_owner(group, block) * depth + row - block * depth, 16), sub)
             is_out = (1 - x // 2).astype(jnp.float32)
             wanted = tgt_t[r, lanes].astype(jnp.float32) * is_out
-            mine = g_block(q, zh * depth, depth, 0)
+            mine = g_block(row0 + zh * sub, sub, 0)
             mine[...] = (keep[0:1, lanes] * (total - wanted)).astype(bf)
             for k in (2, 1, 3):
-                send_g(q, k, mine, z_peer(k) * 4 + x)
+                send(3, mine, mine, z_peer(k) * 4 + x)
         if i == 4:
-            for k in (1, 3, 2):
-                got_g(q, k, g_block(q, z_peer(4 - k) * depth, depth, 0))
-            send_g(q, 4, g_block(q, 0, piece, 0), right)
-            send_g(q, 5, g_block(q, 0, piece, 0), left)
+            came(3, three)
+            ref = g_block(row0, size, 0)
+            send(4, ref, ref, right)
+            send(4, ref, ref, left)
         if i == 5:
-            got_g(q, 4, g_block(q, 0, piece, 3))
-            send_g(q, 6, g_block(q, 0, half, 3), right)
-            got_g(q, 5, g_block(q, 0, piece, 1))
-            send_g(q, 7, g_block(q, half, half, 1), left)
+            came(4, two)
+            ref = g_block(row0, mid, 3)
+            send(5, ref, ref, right)
+            ref = g_block(row0 + mid, mid, 1)
+            send(5, ref, ref, left)
         if i == 6:
-            got_g(q, 6, g_block(q, 0, half, 2))
-            got_g(q, 7, g_block(q, half, half, 2))
-
-    def back_piece(q):
+            came(5, one)
+
+    def back_chunk(group, c):
+        r = slice(group * piece, (group + 1) * piece)
+        term = dot_tn(gt[r], full[r, c])
+        if group == 0:
+            back[:, c] = term
+        else:
+            back[:, c] += term
+
+    def back_piece(group):
         def chunk(n, _):
-            c = pl.ds(pl.multiple_of(n * 384, 128), 384)
-            term = dot_tn(gt[q * piece : (q + 1) * piece], full[q * piece : (q + 1) * piece, c])
-            if q == 0:
-                back[:, c] = term
-            else:
-                back[:, c] += term
+            back_chunk(group, pl.ds(pl.multiple_of(n * part, 128), part))
             return 0
 
-        lax.fori_loop(0, cols // 384, chunk, 0)
+        lax.fori_loop(0, PARTS, chunk, 0)
 
     out_piece(0)
     step(0, 0)
-    out_piece(1)
-    step(0, 1)
     wait(3, 7)
     start(3, 13)
     wait(3, 8)
     start(3, 14, 15)
-    step(1, 0)
-    step(2, 0)
-    diagonal(3)
-    step(1, 1)
+    out_piece(1)
+    step(0, 1)
     out_piece(2)
     step(0, 2)
-    step(2, 1)
-    last(3)
-    step(3, 0)
     out_piece(3)
     step(0, 3)
+    out_piece(4)
+    out_piece(5)
+    step(1, 0)
+    step(0, 5)
+    step(1, 1)
+    diagonal(3)
     step(1, 2)
+    step(0, 4)
+    step(1, 3)
+    step(2, 0)
+    step(1, 5)
+    out_piece(6)
+    step(2, 1)
+    step(0, 6)
+    out_piece(7)
+    last(3)
+    step(2, 2)
+    step(1, 4)
+    out_piece(8)
+    step(0, 8)
+    step(0, 7)
+    step(2, 3)
+    step(2, 5)
+    step(3, 0)
+    step(1, 6)
+    out_piece(9)
+    step(0, 9)
     step(3, 1)
-    step(1, 3)
-    step(2, 2)
+    out_piece(10)
+    step(0, 10)
+    out_piece(11)
+    step(2, 4)
+    step(0, 11)
+    step(3, 3)
+    step(3, 2)
+    step(1, 7)
+    step(1, 8)
+    step(1, 9)
+    step(2, 6)
+    step(3, 5)
     step(4, 0)
+    step(1, 10)
+    step(1, 11)
+    step(3, 4)
     step(4, 1)
-    step(2, 3)
-    step(3, 2)
+    step(2, 7)
+    step(2, 8)
+    step(4, 3)
+    step(4, 2)
+    step(2, 9)
     step(5, 0)
-    step(3, 3)
+    step(2, 11)
+    step(2, 10)
+    step(4, 5)
     step(5, 1)
+    step(4, 4)
+    step(3, 6)
+    step(5, 3)
+    step(3, 8)
+    step(3, 7)
+    step(5, 2)
+    step(3, 9)
+    step(5, 5)
     step(6, 0)
-    step(4, 2)
+    step(6, 1)
+    step(5, 4)
+    step(6, 3)
+    step(3, 10)
+    step(3, 11)
+    step(4, 6)
+    step(6, 2)
+    step(4, 8)
     back_piece(0)
-    step(6, 1)
-    step(4, 3)
+    step(4, 7)
+    step(6, 4)
+    step(4, 9)
+    step(6, 5)
+    step(4, 10)
+    step(4, 11)
+    step(5, 6)
     back_piece(1)
-    step(5, 2)
-    step(5, 3)
-    step(6, 2)
+    step(5, 8)
+    step(5, 7)
+    step(5, 9)
+    step(5, 10)
+    step(5, 11)
+    step(6, 6)
+    step(6, 8)
+    step(6, 7)
     back_piece(2)
-    step(6, 3)
-    back_piece(3)
+    step(6, 9)
+    step(6, 10)
+    step(6, 11)
 
     loads[3].wait()
     loads[4].wait()
@@ -580,10 +658,10 @@
         return cin.at[slot, pl.ds(lo, size), pc(q)]
 
     def send_c(src, dst, k, q, target):
-        go(src, dst, cs.at[q, k], cr.at[q, k], "dp", target)
+        go(src, dst, cs.at[0], cr.at[q, k], "dp", target, False)
 
     def got_c(ref, k, q):
-        got(ref, cs.at[q, k], cr.at[q, k])
+        got(ref, cs.at[0], cr.at[q, k])
 
     rest = depth - cut
 
@@ -633,6 +711,7 @@
             tgg[r, pc(q)] = (fac[0, r, pc(q)] * back[r2, pc(q)] + fac[1, r, pc(q)] * back[r, pc(q)]).astype(bf)
             return 0
 
+        back_chunk(3, pc(q))
         lax.fori_loop(0, tok_rows // 32, combine, 0)
         go(tgg.at[:, pc(q)], tgg2.at[:, pc(q)], ms.at[2 + q], mr.at[2 + q], "dp", sib)
     for q in range(PARTS):
@@ -643,6 +722,14 @@
         reduce_step(2, q)
     for q in range(PARTS):
         reduce_step(3, q)
+    for w in range(4):
+        ref = full if w == 3 else half.at[w]
+        ref = ref.at[pl.ds(0, 15 * depth)]
+        pltpu.make_async_copy(ref, ref, gs.at[w]).wait()
+    ref = full.at[pl.ds(0, width * 15 * 128 // (2 * cols))]
+    pltpu.make_async_copy(ref, ref, sx.at[0]).wait()
+    ref = full.at[pl.ds(0, 7 * depth)]
+    pltpu.make_async_copy(ref, ref, cs.at[0]).wait()
     for copy in sent:
         copy.wait_send()
 
@@ -678,10 +765,10 @@
         vm((width, 2 * tok_rows), bf),
         vm((2 * tok_rows, cols), f32),
         vm((width, 2 * tok_rows), bf),
-        vm((4, 3, piece, 128), bf),
-        vm((4, piece, 128), bf),
-        vm((4, piece, 128), bf),
-        vm((4, 3, depth, 128), bf),
+        vm((3, width, 128), bf),
+        vm((width, 128), bf),
+        vm((width, 128), bf),
+        vm((3, width // 4, 128), bf),
         vm((tok_rows, cols), bf),
         vm((tok_rows, cols), bf),
         vm((8 * depth, cols), bf),
@@ -689,15 +776,11 @@
         vm((4, depth, cols), bf),
         vm((depth, cols), bf),
         vm((depth, cols), bf),
+        dma((4,)),
         dma((4, GATHER_COPIES)),
-        dma((4, GATHER_COPIES)),
-        dma((4, 6)),
-        dma((4, 6)),
-        dma((4, 6)),
-        dma((4, 6)),
-        dma((4, 8)),
-        dma((4, 8)),
-        dma((PARTS, 8)),
+        dma((1,)),
+        dma((len(PIECES), 6)),
+        dma((1,)),
         dma((PARTS, 8)),
         dma((2 + PARTS,)),
         dma((2 + PARTS,)),

time: 145 us -> 137 us (0.945)
  Pallas kernels: 143 us -> 134 us
    pallas_call x1, Pallas kernels: 143 us -> 134 us  [per_device(): pl.pallas_call(functools.partial(step_kernel, (tok_rows, width, depth, co...]
where the time goes in v5:
time: 137 us; the launch traced here: 136 us
  Pallas kernels  134 us (98%)
  local copies, waits for them, and re-layouts  1.73 us (1%)
    pallas_call x1, Pallas kernels, per_device(): pl.pallas_call(functools.partial(step_kernel, (tok_rows, width, depth, co...  134 us

profile of v5, /device:TPU:1, one launch (start us, length us, event | category | flops | bytes accessed | tf_op | source)
XLA Modules:
  0.0 135.6 jit_solution(9046630076991109369)
XLA Ops:
  0.0 133.9 %shard_map.82 = bf16[144,1152]{1,0:T(8,128)(2,1)} custom-call(bf16[256,2304]{1,0:T(8,128)(2,1)} %tok_hbm.1, bf16[256,2304]{1,0:T(8,128)(2,1)} %tgt_hbm.1, s32[1,256]{1,0:T(1,128)} %bitcast.1, bf16[144,1152]{1,0:T(8,128)(2,1)} %gate_hbm.1, bf16[144,1152]{1,0:T(8,128)(2,1)} %up_hbm.1, bf16[144,1152]{1,0:T(8,128)(2,1)} %vec_hbm.1, bf16[144,1152]{1,0:T(8,128)(2,1)} %down_hbm.1, ...), custom_call_target="tpu_custom_call" | custom-call | tf_op jit(solution)/shard_map/pallas_call | solution.py:791
  133.9 1.7 %copy.10 = bf16[144,1152]{1,0:T(8,128)(2,1)} copy(bf16[144,1152]{1,0:T(8,128)(2,1)} %shard_map.82) | data formatting | bytes 663552

commit v6 on v5

--- a/solution.py
+++ b/solution.py
@@ -40,7 +40,7 @@
 
 
 GATHER_COPIES = 19
-PARTS = 3
+PARTS = ((0, 256), (256, 384), (640, 256), (896, 256))
 PIECES = ((0, 4), (4, 4), (8, 4), (12, 4), (16, 4), (20, 4), (24, 4), (28, 4), (32, 4), (36, 4), (40, 4), (44, 4))
 
 
@@ -78,7 +78,7 @@
     cut = (depth // 32 + 1) * 16
     wide = -(-cols // 256) * 128
     rem = cols - wide
-    part = cols // PARTS
+    third = cols // 3
     inv_root = float(width) ** (-0.5)
 
     def at(dy, dz, dc):
@@ -311,9 +311,9 @@
     loads[1].wait()
     turn(tgt, tgt_t)
     tokens_start()
+    near_z(1)
     round_z(0)
     near(1)
-    near_z(1)
     use(0, 0)
     far(0)
     use(0, -1)
@@ -524,10 +524,10 @@
 
     def back_piece(group):
         def chunk(n, _):
-            back_chunk(group, pl.ds(pl.multiple_of(n * part, 128), part))
+            back_chunk(group, pl.ds(pl.multiple_of(n * third, 128), third))
             return 0
 
-        lax.fori_loop(0, PARTS, chunk, 0)
+        lax.fori_loop(0, 3, chunk, 0)
 
     out_piece(0)
     step(0, 0)
@@ -640,7 +640,7 @@
     got(tok_t2, ms.at[1], mr.at[1])
 
     def pc(q):
-        return pl.ds(q * part, part)
+        return pl.ds(*PARTS[q])
 
     def chip(dy, dz):
         return at(dy, dz, 0) // 2
@@ -663,32 +663,50 @@
     def got_c(ref, k, q):
         got(ref, cs.at[0], cr.at[q, k])
 
-    rest = depth - cut
+    rest, via_z = depth - cut, 16
+    keep_y = depth - via_z
 
     def reduce_step(i, q):
         if i == 0:
             got(tgg2.at[:, pc(q)], ms.at[2 + q], mr.at[2 + q])
             make(q, (2, 1), (1, 1), (-1, 1))
             send_c(c_block(2, 1, q), box(0, q), 0, q, zed)
-            send_c(c_block(1, 1, q), box(1, q), 1, q, up)
-            send_c(c_block(-1, 1, q), box(2, q), 2, q, down)
+            send_c(c_block(1, 1, q, 0, keep_y), box(1, q, 0, keep_y), 1, q, up)
+            send_c(c_block(-1, 1, q, 0, keep_y), box(2, q, 0, keep_y), 2, q, down)
+            send_c(c_block(1, 1, q, keep_y, via_z), box(1, q, keep_y, via_z), 8, q, zed)
+            send_c(c_block(-1, 1, q, keep_y, via_z), box(2, q, keep_y, via_z), 9, q, zed)
             make(q, (2, 0), (0, 1), (1, 0), (-1, 0), (0, 0))
         if i == 1:
             got_c(box(0, q), 0, q)
             cout[0, :, pc(q)] = plus(c_block(2, 0, q)[...], box(0, q)[...]).astype(bf)
             send_c(cout.at[0, pl.ds(0, cut), pc(q)], box(3, q, 0, cut), 3, q, up)
             send_c(cout.at[0, pl.ds(cut, rest), pc(q)], box(3, q, cut, rest), 4, q, down)
-            got_c(box(1, q), 1, q)
-            got_c(box(2, q), 2, q)
-            cout[1, :, pc(q)] = plus(c_block(0, 1, q)[...], box(1, q)[...], box(2, q)[...]).astype(bf)
+            got_c(box(1, q, 0, keep_y), 1, q)
+            got_c(box(2, q, 0, keep_y), 2, q)
+            cout[1, :keep_y, pc(q)] = plus(
+                c_block(0, 1, q, 0, keep_y)[...], box(1, q, 0, keep_y)[...], box(2, q, 0, keep_y)[...]
+            ).astype(bf)
+            cout[1, keep_y:, pc(q)] = c_block(0, 1, q, keep_y, via_z)[...]
             send_c(cout.at[1, :, pc(q)], box(4, q), 5, q, zed)
         if i == 2:
             got_c(box(3, q, 0, cut), 3, q)
             cout[2, :cut, pc(q)] = plus(c_block(1, 0, q, 0, cut)[...], box(3, q, 0, cut)[...]).astype(bf)
-            cout[2, cut:, pc(q)] = c_block(1, 0, q, cut, rest)[...]
+            got_c(box(1, q, keep_y, via_z), 8, q)
+            got_c(box(2, q, keep_y, via_z), 9, q)
+            cout[2, cut:keep_y, pc(q)] = c_block(1, 0, q, cut, keep_y - cut)[...]
+            cout[2, keep_y:, pc(q)] = plus(
+                c_block(1, 0, q, keep_y, via_z)[...], box(1, q, keep_y, via_z)[...]
+            ).astype(bf)
             send_c(cout.at[2, :, pc(q)], box(5, q), 6, q, up)
             got_c(box(3, q, cut, rest), 4, q)
-            cout[3, cut:, pc(q)] = plus(c_block(-1, 0, q, cut, rest)[...], box(3, q, cut, rest)[...]).astype(bf)
+            cout[3, cut:keep_y, pc(q)] = plus(
+                c_block(-1, 0, q, cut, keep_y - cut)[...], box(3, q, cut, keep_y - cut)[...]
+            ).astype(bf)
+            cout[3, keep_y:, pc(q)] = plus(
+                c_block(-1, 0, q, keep_y, via_z)[...],
+                box(3, q, keep_y, via_z)[...],
+                box(2, q, keep_y, via_z)[...],
+            ).astype(bf)
             cout[3, :cut, pc(q)] = c_block(-1, 0, q, 0, cut)[...]
             send_c(cout.at[3, :, pc(q)], box(6, q), 7, q, down)
         if i == 3:
@@ -703,7 +721,7 @@
                 - step_size * total
             ).astype(bf)
 
-    for q in range(PARTS):
+    for q in range(len(PARTS)):
 
         def combine(i, _):
             r = pl.ds(pl.multiple_of(i * 32, 16), 32)
@@ -714,13 +732,13 @@
         back_chunk(3, pc(q))
         lax.fori_loop(0, tok_rows // 32, combine, 0)
         go(tgg.at[:, pc(q)], tgg2.at[:, pc(q)], ms.at[2 + q], mr.at[2 + q], "dp", sib)
-    for q in range(PARTS):
+    for q in range(len(PARTS)):
         reduce_step(0, q)
-    for q in range(PARTS):
+    for q in range(len(PARTS)):
         reduce_step(1, q)
-    for q in range(PARTS):
+    for q in range(len(PARTS)):
         reduce_step(2, q)
-    for q in range(PARTS):
+    for q in range(len(PARTS)):
         reduce_step(3, q)
     for w in range(4):
         ref = full if w == 3 else half.at[w]
@@ -781,9 +799,9 @@
         dma((1,)),
         dma((len(PIECES), 6)),
         dma((1,)),
-        dma((PARTS, 8)),
-        dma((2 + PARTS,)),
-        dma((2 + PARTS,)),
+        dma((len(PARTS), 10)),
+        dma((2 + len(PARTS),)),
+        dma((2 + len(PARTS),)),
         dma((8,)),
         dma((8,)),
         dma((9,)),
@@ -795,7 +813,7 @@
         out_specs=pl.BlockSpec(memory_space=pltpu.VMEM),
         scratch_shapes=scratch,
         compiler_params=pltpu.CompilerParams(
-            collective_id=1, has_side_effects=True, vmem_limit_bytes=56 * 2**20
+            collective_id=1, has_side_effects=True, vmem_limit_bytes=107 * 2**19
         ),
     )(tokens, target, segments[None], gate_weight, up_weight, vector, down_weight, gradient)
 

time: 137 us -> 135 us (0.985)
  no operation moved by 1% of the time
where the time goes in v6:
time: 135 us
  Pallas kernels  133 us (99%)
  local copies, waits for them, and re-layouts  1.41 us (1%)
    pallas_call x1, Pallas kernels, per_device(): pl.pallas_call(functools.partial(step_kernel, (tok_rows, width, depth, co...  133 us

profile of v6, /device:TPU:1, one launch (start us, length us, event | category | flops | bytes accessed | tf_op | source)
XLA Modules:
  0.0 134.6 jit_solution(9371427313361167256)
XLA Ops:
  0.0 0.0 copy-start
  0.0 0.7 copy-done
  0.7 133.2 %shard_map.82 = bf16[144,1152]{1,0:T(8,128)(2,1)S(1)} custom-call(bf16[256,2304]{1,0:T(8,128)(2,1)} %tok_hbm.1, bf16[256,2304]{1,0:T(8,128)(2,1)} %tgt_hbm.1, s32[1,256]{1,0:T(1,128)S(1)} %bitcast.1, bf16[144,1152]{1,0:T(8,128)(2,1)} %gate_hbm.1, bf16[144,1152]{1,0:T(8,128)(2,1)} %up_hbm.1, bf16[144,1152]{1,0:T(8,128)(2,1)} %vec_hbm.1, ...), custom_call_target="tpu_custom_call" | custom-call | tf_op jit(solution)/shard_map/pallas_call | solution.py:809
  133.9 0.7 copy.10
Async XLA Ops:
  0.0 0.7 copy-start

commit v7 on v6

--- a/solution.py
+++ b/solution.py
@@ -40,7 +40,7 @@
 
 
 GATHER_COPIES = 19
-PARTS = ((0, 256), (256, 384), (640, 256), (896, 256))
+PARTS = ((0, 128), (128, 384), (512, 384), (896, 256))
 PIECES = ((0, 4), (4, 4), (8, 4), (12, 4), (16, 4), (20, 4), (24, 4), (28, 4), (32, 4), (36, 4), (40, 4), (44, 4))
 
 
@@ -529,111 +529,111 @@
 
         lax.fori_loop(0, 3, chunk, 0)
 
-    out_piece(0)
-    step(0, 0)
+    out_piece(5)
+    step(0, 5)
     wait(3, 7)
     start(3, 13)
     wait(3, 8)
     start(3, 14, 15)
+    out_piece(0)
+    step(0, 0)
     out_piece(1)
+    out_piece(3)
+    step(0, 3)
     step(0, 1)
     out_piece(2)
+    step(1, 5)
+    step(1, 0)
     step(0, 2)
-    out_piece(3)
-    step(0, 3)
     out_piece(4)
-    out_piece(5)
-    step(1, 0)
-    step(0, 5)
+    diagonal(3)
+    step(1, 3)
     step(1, 1)
-    diagonal(3)
-    step(1, 2)
+    step(2, 5)
     step(0, 4)
-    step(1, 3)
     step(2, 0)
-    step(1, 5)
-    out_piece(6)
-    step(2, 1)
-    step(0, 6)
-    out_piece(7)
-    last(3)
-    step(2, 2)
-    step(1, 4)
     out_piece(8)
     step(0, 8)
+    out_piece(6)
+    step(0, 6)
+    step(2, 3)
+    last(3)
+    out_piece(7)
+    step(1, 2)
     step(0, 7)
-    step(2, 3)
-    step(2, 5)
+    step(2, 1)
+    step(1, 4)
+    step(3, 5)
     step(3, 0)
-    step(1, 6)
+    step(1, 8)
     out_piece(9)
     step(0, 9)
+    step(3, 3)
+    out_piece(11)
+    step(1, 6)
+    step(2, 2)
+    step(0, 11)
     step(3, 1)
     out_piece(10)
+    step(2, 4)
+    step(1, 7)
     step(0, 10)
-    out_piece(11)
-    step(2, 4)
-    step(0, 11)
-    step(3, 3)
+    step(4, 5)
+    step(2, 6)
+    step(2, 8)
+    step(1, 9)
+    step(4, 0)
+    step(2, 7)
     step(3, 2)
-    step(1, 7)
-    step(1, 8)
-    step(1, 9)
-    step(2, 6)
-    step(3, 5)
-    step(4, 0)
     step(1, 10)
     step(1, 11)
+    step(5, 5)
     step(3, 4)
     step(4, 1)
-    step(2, 7)
-    step(2, 8)
+    step(3, 6)
+    step(2, 10)
+    step(3, 8)
+    step(2, 11)
     step(4, 3)
+    step(5, 0)
+    step(3, 7)
+    step(6, 5)
     step(4, 2)
+    step(4, 4)
     step(2, 9)
-    step(5, 0)
-    step(2, 11)
-    step(2, 10)
-    step(4, 5)
     step(5, 1)
-    step(4, 4)
-    step(3, 6)
+    step(4, 6)
     step(5, 3)
-    step(3, 8)
-    step(3, 7)
+    step(6, 0)
+    step(3, 10)
+    step(4, 8)
     step(5, 2)
-    step(3, 9)
-    step(5, 5)
-    step(6, 0)
+    step(3, 11)
+    step(4, 7)
     step(6, 1)
     step(5, 4)
+    step(3, 9)
+    step(5, 6)
+    step(4, 10)
     step(6, 3)
-    step(3, 10)
-    step(3, 11)
-    step(4, 6)
+    step(5, 8)
     step(6, 2)
-    step(4, 8)
+    step(4, 11)
     back_piece(0)
-    step(4, 7)
+    step(4, 9)
+    step(5, 7)
     step(6, 4)
-    step(4, 9)
-    step(6, 5)
-    step(4, 10)
-    step(4, 11)
-    step(5, 6)
     back_piece(1)
-    step(5, 8)
-    step(5, 7)
-    step(5, 9)
+    step(6, 8)
+    step(6, 6)
     step(5, 10)
     step(5, 11)
-    step(6, 6)
-    step(6, 8)
+    step(5, 9)
     step(6, 7)
     back_piece(2)
+    step(6, 11)
+    step(6, 10)
     step(6, 9)
-    step(6, 10)
-    step(6, 11)
 
     loads[3].wait()
     loads[4].wait()

time: 135 us -> 134 us (level)
  no operation moved by 1% of the time
where the time goes in v7:
time: 134 us
  Pallas kernels  132 us (99%)
  local copies, waits for them, and re-layouts  1.41 us (1%)
    pallas_call x1, Pallas kernels, per_device(): pl.pallas_call(functools.partial(step_kernel, (tok_rows, width, depth, co...  132 us

profile of v7, /device:TPU:1, one launch (start us, length us, event | category | flops | bytes accessed | tf_op | source)
XLA Modules:
  0.0 133.7 jit_solution(12208580008538842930)
XLA Ops:
  0.0 0.0 copy-start
  0.0 0.7 copy-done
  0.7 132.2 %shard_map.82 = bf16[144,1152]{1,0:T(8,128)(2,1)S(1)} custom-call(bf16[256,2304]{1,0:T(8,128)(2,1)} %tok_hbm.1, bf16[256,2304]{1,0:T(8,128)(2,1)} %tgt_hbm.1, s32[1,256]{1,0:T(1,128)S(1)} %bitcast.1, bf16[144,1152]{1,0:T(8,128)(2,1)} %gate_hbm.1, bf16[144,1152]{1,0:T(8,128)(2,1)} %up_hbm.1, bf16[144,1152]{1,0:T(8,128)(2,1)} %vec_hbm.1, ...), custom_call_target="tpu_custom_call" | custom-call | tf_op jit(solution)/shard_map/pallas_call | solution.py:809
  132.9 0.7 copy.10
Async XLA Ops:
  0.0 0.7 copy-start

commit v8 on v7

--- a/solution.py
+++ b/solution.py
@@ -40,7 +40,7 @@
 
 
 GATHER_COPIES = 19
-PARTS = ((0, 128), (128, 384), (512, 384), (896, 256))
+PARTS = ((0, 128), (128, 384), (512, 512), (1024, 128))
 PIECES = ((0, 4), (4, 4), (8, 4), (12, 4), (16, 4), (20, 4), (24, 4), (28, 4), (32, 4), (36, 4), (40, 4), (44, 4))
 
 

time: 134 us -> 134 us (level)
  no operation moved by 1% of the time
where the time goes in v8:
time: 134 us
  Pallas kernels  133 us (99%)
  local copies, waits for them, and re-layouts  1.41 us (1%)
    pallas_call x1, Pallas kernels, per_device(): pl.pallas_call(functools.partial(step_kernel, (tok_rows, width, depth, co...  133 us

profile of v8, /device:TPU:1, one launch (start us, length us, event | category | flops | bytes accessed | tf_op | source)
XLA Modules:
  0.0 134.2 jit_solution(2867310546682184403)
XLA Ops:
  0.0 0.0 copy-start
  0.0 0.7 copy-done
  0.7 132.8 %shard_map.82 = bf16[144,1152]{1,0:T(8,128)(2,1)S(1)} custom-call(bf16[256,2304]{1,0:T(8,128)(2,1)} %tok_hbm.1, bf16[256,2304]{1,0:T(8,128)(2,1)} %tgt_hbm.1, s32[1,256]{1,0:T(1,128)S(1)} %bitcast.1, bf16[144,1152]{1,0:T(8,128)(2,1)} %gate_hbm.1, bf16[144,1152]{1,0:T(8,128)(2,1)} %up_hbm.1, bf16[144,1152]{1,0:T(8,128)(2,1)} %vec_hbm.1, ...), custom_call_target="tpu_custom_call" | custom-call | tf_op jit(solution)/shard_map/pallas_call | solution.py:809
  133.4 0.7 copy.10
Async XLA Ops:
  0.0 0.7 copy-start
